TPU v7x, 32 devices: a whole 2x2x4 slice. The times are simulated.
32 devices in a mesh: lon: 16 (over z, x, core), lat: 2 (over y).
Axes of the slice: x: 2, y: 2, z: 4, core: 2. Of those that a mesh axis runs over, the one named last changes fastest.
Arguments:
- earlier_state: float32 [4, 4, 128, 8192], P(None, None, 'lat', 'lon'), may hold values from -6 to 6
- present_state: float32 [4, 4, 128, 8192], P(None, None, 'lat', 'lon'), may hold values from -6 to 6
- scalar_wet_flags: int32 [4, 128, 8192], P(None, 'lat', 'lon'), may hold values 0 or 1
- eastside_wet_flags: int32 [4, 128, 8192], P(None, 'lat', 'lon'), may hold values 0 or 1
- northside_wet_flags: int32 [4, 128, 8192], P(None, 'lat', 'lon'), may hold values 0 or 1
Outputs:
- after: float32 [4, 4, 128, 8192], P(None, None, 'lat', 'lon')
- filtered: float32 [4, 4, 128, 8192], P(None, None, 'lat', 'lon')
All inputs are finite; a program needn't handle non-finite values. No bound on the sum of `scalar_wet_flags` or of `eastside_wet_flags` or of `northside_wet_flags` on one device may be relied on, other than what follows from the above.
Results may differ from a plain program's by a relative error of at most 0.00002.
Values sent between devices are 32-bit elements; how exact they have to be, the bound alone decides.
No kernel may reach another device: no remote copies, remote signals or barrier semaphores. Data moves between devices by JAX's collectives and lax.ppermute only.
A program may use at most 128 MiB of HBM per device.

v0:
```python
import jax
import jax.numpy as jnp
from jax import lax
from jax.sharding import PartitionSpec as P

advect_coef = 0.5
diffuse_coef = 0.25
twice_step = 0.5
gravity = 0.5
coriolis = 0.5
thermal = 0.2
haline = 0.15
asselin = 0.1


def from_partner(x, axis, stride):
    return lax.ppermute(x, axis, [(i, i ^ 1 << stride) for i in range(lax.axis_size(axis))])


def passed_along(x, axis, by):
    length = lax.axis_size(axis)
    return lax.ppermute(x, axis, [(i, (i + by) % length) for i in range(length)])


def passed_along_2(x, axis, by):
    length = lax.axis_size(axis)
    pairs = [(i, i + by) for i in range(length) if 0 <= i + by < length]
    return lax.ppermute(x, axis, pairs)


def pressure(temp, salt):
    density = haline * salt - thermal * temp
    return jnp.cumsum(density, axis=0) - 0.5 * density


def face_flux(here, ahead, speed, face_mask):
    return advect_coef * speed * (here[:4] + ahead[:4]) * 0.5 - diffuse_coef * face_mask * (
        ahead[4:] - here[4:]
    )


def shards(earlier_state, present_state, scalar_wet_flags, eastside_wet_flags, northside_wet_flags):
    tracer_cell_mask = scalar_wet_flags.astype(jnp.float32)
    mask_u = eastside_wet_flags.astype(jnp.float32)
    southnorth_wet_flags = northside_wet_flags.astype(jnp.float32)
    fmask = jnp.stack([tracer_cell_mask, tracer_cell_mask, mask_u, southnorth_wet_flags])
    curm = present_state * fmask
    befm = earlier_state * fmask
    both = jnp.concatenate([curm, befm], 0)
    height = both.shape[2]
    signs = jnp.array([1.0, 1.0, -1.0, -1.0, 1.0, 1.0, -1.0, -1.0], jnp.float32)[:, None, None]
    top_rows = both[:, :, -1, :]
    mirror = top_rows
    for bit in range(lax.axis_size("lon").bit_length() - 1):
        mirror = from_partner(mirror, "lon", bit)
    mirror = mirror[..., ::-1]
    ghost = mirror * signs
    is_top = lax.axis_index("lat") == lax.axis_size("lat") - 1
    east_col = passed_along(both[:, :, :, :1], "lon", -1)
    east = jnp.concatenate([both[:, :, :, 1:], east_col], 3)
    above_row = passed_along_2(both[:, :, :1, :], "lat", -1)
    north_row = jnp.where(is_top, ghost, above_row[:, :, 0, :])
    north = jnp.concatenate([both[:, :, 1:, :], north_row[:, :, None, :]], 2)
    flux_e = face_flux(both, east, curm[2], mask_u)
    northern_face_flux = face_flux(both, north, curm[3], southnorth_wet_flags)
    west_col = passed_along(flux_e[:, :, :, -1:], "lon", 1)
    flux_w = jnp.concatenate([west_col, flux_e[:, :, :, :-1]], 3)
    south_row = passed_along_2(northern_face_flux[:, :, -1:, :], "lat", 1)
    flux_s = jnp.concatenate([south_row, northern_face_flux[:, :, :-1, :]], 2)
    pres = pressure(curm[0], curm[1])
    pres_e = pressure(east[0], east[1])
    pres_n = pressure(north[0], north[1])
    global_rows = (lax.axis_index("lat") * height + jnp.arange(height, dtype=jnp.int32)).astype(
        jnp.float32
    )
    total_rows = height * lax.axis_size("lat")
    cor = (coriolis * (2.0 * (global_rows + 0.5) / total_rows - 1.0))[:, None]
    tend = -(flux_e - flux_w + (northern_face_flux - flux_s))
    zonal_velocity_tendency = tend[2] + (cor * curm[3] - gravity * mask_u * (pres_e - pres))
    tend_v = tend[3] - (cor * curm[2] + gravity * southnorth_wet_flags * (pres_n - pres))
    tend = jnp.stack([tend[0], tend[1], zonal_velocity_tendency, tend_v])
    after = (befm + twice_step * tend) * fmask
    filtered = curm + asselin * (befm - 2.0 * curm + after)
    return (after, filtered)


def solution(mesh):
    placed = (
        P(None, None, "lat", "lon"),
        P(None, None, "lat", "lon"),
        P(None, "lat", "lon"),
        P(None, "lat", "lon"),
        P(None, "lat", "lon"),
    )
    return jax.shard_map(
        shards,
        mesh=mesh,
        in_specs=placed,
        out_specs=(P(None, None, "lat", "lon"), P(None, None, "lat", "lon")),
        check_vma=False,
    )
```

profile of v0, /device:TPU:0, one launch (start us, length us, event | category | flops | bytes accessed | tf_op | source)
XLA Modules:
  0.0 82.6 jit_solution(17568572561123046763)
XLA Ops:
  0.6 1.2 %convert_bitcast_fusion.2 = f32[1,4,64,512]{3,2,1,0:T(8,128)S(1)} fusion(s32[4,64,512]{2,1,0:T(8,128)} %param.8), kind=kLoop, calls=%fused_computation.80 | loop fusion | flops 131072 | bytes 1048576 | tf_op jit(solution)/shard_map/stack | solution.py:46
  1.9 1.5 %convert_bitcast_fusion = (f32[1,4,64,512]{3,2,1,0:T(8,128)S(1)}, f32[1,4,64,512]{3,2,1,0:T(8,128)S(1)}) fusion(s32[4,64,512]{2,1,0:T(8,128)} %param.10, s32[4,64,512]{2,1,0:T(8,128)} %param.9), kind=kLoop, calls=%fused_computation.77 | loop fusion | flops 262144 | bytes 2097152 | tf_op jit(solution)/shard_map/stack | solution.py:46
  3.4 2.7 %fusion.27 = (f32[4,4,64,512]{3,2,1,0:T(8,128)S(1)}, f32[4,4,64,512]{3,2,1,0:T(8,128)S(1)}) fusion(f32[4,4,64,512]{3,2,1,0:T(8,128)S(1)} %copy-done.16, f32[1,4,64,512]{3,2,1,0:T(8,128)S(1)} %get-tuple-element.18, f32[1,4,64,512]{3,2,1,0:T(8,128)S(1)} %get-tuple-element.19, f32[1,4,64,512]{3,2,1,0:T(8,128)S(1)} %convert_bitcast_fusion.2, ...), kind=kLoop, calls=%fused_computation.49 | loop fusion | flops 2621440 | bytes 9961472 | tf_op jit(solution)/shard_map/mul | solution.py:48
  6.1 1.4 %copy_dynamic-update-slice_fusion.1 = f32[8,4,64,512]{3,1,0,2:T(4,128)S(1)} fusion(f32[4,4,64,512]{3,2,1,0:T(8,128)S(1)} %get-tuple-element.17), kind=kLoop, calls=%fused_computation.37 | loop fusion | bytes 4194304
  7.5 1.5 %copy_dynamic-update-slice_fusion = f32[8,4,64,512]{3,1,0,2:T(4,128)S(1)} fusion(f32[8,4,64,512]{3,1,0,2:T(4,128)S(1)} %copy_dynamic-update-slice_fusion.1, f32[4,4,64,512]{3,2,1,0:T(8,128)S(1)} %get-tuple-element.16), kind=kLoop, calls=%fused_computation.36 | loop fusion | bytes 4194304 | tf_op jit(solution)/shard_map/concatenate | solution.py:49
  9.0 0.5 collective-permute-start.2
  9.6 1.4 %collective-permute-start.6 = (f32[8,4,1,512]{3,1,0,2:T(4,128)S(1)}, f32[8,4,1,512]{3,1,0,2:T(4,128)S(1)}, u32[]{:S(2)}, u32[]{:S(2)}) collective-permute-start(f32[8,4,1,512]{3,1,0,2:T(4,128)S(1)} %get-tuple-element.11), channel_id=1, source_target_pairs={{1,0},{3,2},{5,4},{7,6},{9,8},{11,10},{13,12},{15,14},{17,16},{19,... | collective-permute-start | bytes 196616 | tf_op jit(solution)/shard_map/ppermute | solution.py:28
  11.0 1.2 %slice.102 = f32[8,4,64,1]{3,1,0,2:T(4,128)} slice(f32[8,4,64,512]{3,1,0,2:T(4,128)S(1)} %copy_dynamic-update-slice_fusion), slice={[0:8], [0:4], [0:64], [0:1]} | slice | bytes 16384 | tf_op jit(solution)/shard_map/slice | solution.py:59
  12.2 1.8 %copy.47 = f32[8,4,64,1]{2,0,3,1:T(8,128)S(1)} copy(f32[8,4,64,1]{3,1,0,2:T(4,128)} %slice.102) | data formatting | bytes 16384 | tf_op jit(solution)/shard_map/slice | solution.py:59
  13.9 5.8 %collective-permute-start = (f32[8,4,64,1]{2,0,3,1:T(8,128)S(1)}, f32[8,4,64,1]{2,0,3,1:T(8,128)S(1)}, u32[]{:S(2)}, u32[]{:S(2)}) collective-permute-start(f32[8,4,64,1]{2,0,3,1:T(8,128)S(1)} %copy.47), channel_id=1, source_target_pairs={{0,30},{2,0},{4,2},{6,4},{8,6},{10,8},{12,10},{14,12},{16,14},{18,... | collective-permute-start | bytes 24584 | tf_op jit(solution)/shard_map/ppermute | solution.py:22
  19.8 1.1 %convert_multiply_fusion = (f32[4,64,512]{2,1,0:T(8,128)}, f32[4,64,512]{2,1,0:T(8,128)}) fusion(s32[4,64,512]{2,1,0:T(8,128)S(1)} %copy-done.14, s32[4,64,512]{2,1,0:T(8,128)S(1)} %copy-done.12), kind=kLoop, calls=%fused_computation.76 | loop fusion | flops 524288 | bytes 2097152 | tf_op jit(solution)/shard_map/mul | solution.py:37
  20.9 1.1 %multiply_bitcast_fusion = (f32[4,64,512]{2,1,0:T(8,128)}, f32[4,64,512]{2,1,0:T(8,128)}) fusion(f32[4,4,64,512]{3,2,1,0:T(8,128)S(1)} %get-tuple-element.17), kind=kLoop, calls=%fused_computation.74 | loop fusion | flops 262144 | bytes 2097152 | tf_op jit(solution)/shard_map/mul | solution.py:37
  22.0 0.9 %reduce-window_subtract_fusion.1 = f32[4,64,512]{2,1,0:T(8,128)} fusion(f32[4,4,64,512]{3,2,1,0:T(8,128)S(1)} %get-tuple-element.17), kind=kOutput, calls=%fused_computation.40 | output fusion | flops 1441792 | bytes 2621440 | tf_op jit(solution)/shard_map/jit(cumsum)/reduce_window_sum | solution.py:33
  22.9 3.4 %collective-permute-done.3 = f32[8,4,512]{2,1,0:T(4,128)S(1)} collective-permute-done((f32[8,4,512]{2,1,0:T(4,128)S(1)}, f32[8,4,512]{2,1,0:T(4,128)S(1)}, u32[]{:S(2)}, u32[]{:S(2)}) %collective-permute-start.3) | collective-permute-done | bytes 65568 | tf_op jit(solution)/shard_map/ppermute | solution.py:17
  26.3 5.6 %slice.110 = f32[8,4,63,512]{3,1,0,2:T(4,128)} slice(f32[8,4,64,512]{3,1,0,2:T(4,128)} %copy-done.3), slice={[0:8], [0:4], [1:64], [0:512]} | slice | bytes 8257536 | tf_op jit(solution)/shard_map/slice | solution.py:63
  31.8 4.2 %slice.101 = f32[8,4,64,511]{3,1,0,2:T(4,128)} slice(f32[8,4,64,512]{3,1,0,2:T(4,128)S(1)} %copy-done.4), slice={[0:8], [0:4], [0:64], [1:512]} | slice | bytes 8372224 | tf_op jit(solution)/shard_map/slice | solution.py:60
  36.1 6.7 %copy.48 = f32[8,4,64,511]{3,2,1,0:T(8,128)} copy(f32[8,4,64,511]{3,1,0,2:T(4,128)} %slice.101) | data formatting | bytes 8372224 | tf_op jit(solution)/shard_map/slice | solution.py:60
  42.8 4.4 %copy.52 = f32[8,4,63,512]{3,2,1,0:T(8,128)} copy(f32[8,4,63,512]{3,1,0,2:T(4,128)S(1)} %copy-done.5) | data formatting | bytes 8257536 | tf_op jit(solution)/shard_map/slice | solution.py:63
  47.2 0.4 copy.49
  47.6 1.1 %collective-permute-start.5 = (f32[8,4,512]{2,1,0:T(4,128)S(1)}, f32[8,4,512]{2,1,0:T(4,128)S(1)}, u32[]{:S(2)}, u32[]{:S(2)}) collective-permute-start(f32[8,4,512]{2,1,0:T(4,128)S(1)} %collective-permute-done.4), channel_id=1, source_target_pairs={{0,16},{2,18},{4,20},{6,22},{8,24},{10,26},{12,28},{14,30},{16,0},... | collective-permute-start | bytes 196616 | tf_op jit(solution)/shard_map/ppermute | solution.py:17
  48.7 3.1 %fusion.24 = f32[4,64,512]{2,1,0:T(8,128)} fusion(f32[4,64,512]{2,1,0:T(8,128)} %reduce-window_subtract_fusion.1, f32[8,4,64,1]{3,2,1,0:T(8,128)S(1)} %copy.49, f32[8,4,64,511]{3,2,1,0:T(8,128)} %copy.48, s32[4,64,512]{2,1,0:T(8,128)} %param.9, f32[4,4,64,512]{3,2,1,0:T(8,128)S(1)} %get-tuple-element.17, f32[64]{0:T(128)S(1)} %add_multiply_fusion), kind=kOutput, calls=%fused_computation.46 | output fusion | flops 2752512 | bytes 12583424 | tf_op jit(solution)/shard_map/jit(cumsum)/reduce_window_sum | solution.py:33
  51.8 1.1 %collective-permute-done.5 = f32[8,4,512]{2,1,0:T(4,128)S(1)} collective-permute-done((f32[8,4,512]{2,1,0:T(4,128)S(1)}, f32[8,4,512]{2,1,0:T(4,128)S(1)}, u32[]{:S(2)}, u32[]{:S(2)}) %collective-permute-start.5) | collective-permute-done | bytes 65568 | tf_op jit(solution)/shard_map/ppermute | solution.py:17
  52.9 0.4 rev.3
  53.5 5.8 %fusion.4 = (f32[4,4,64,512]{3,2,1,0:T(8,128)S(1)}, f32[4,4,64,512]{3,2,1,0:T(8,128)S(1)}) fusion(f32[4,4,64,512]{3,2,1,0:T(8,128)S(1)} %get-tuple-element.17, f32[8,4,63,512]{3,2,1,0:T(8,128)} %copy.52, f32[4,4,64,512]{3,2,1,0:T(8,128)} %copy-done.1, f32[8,4,1,512]{3,2,1,0:T(1,128)S(1)} %broadcast_in_dim.2, f32[4,64,512]{2,1,0:T(8,128)} %get-tuple-element.20, ...), kind=kLoop, calls=%fused_computation.16 | loop fusion | flops 8388608 | bytes 18874368 | tf_op jit(solution)/shard_map/sub | solution.py:37
  59.4 4.3 %collective-permute-start.7 = (f32[4,4,1,512]{3,2,1,0:T(1,128)S(1)}, f32[4,4,1,512]{3,2,1,0:T(1,128)S(1)}, u32[]{:S(2)}, u32[]{:S(2)}) collective-permute-start(f32[4,4,1,512]{3,2,1,0:T(1,128)S(1)} %slice.117), channel_id=1, source_target_pairs={{0,1},{2,3},{4,5},{6,7},{8,9},{10,11},{12,13},{14,15},{16,17},{18,... | collective-permute-start | bytes 98312 | tf_op jit(solution)/shard_map/ppermute | solution.py:28
  63.9 0.3 collective-permute-start.1
  64.2 0.2 fusion.25
  64.4 11.0 %collective-permute-done.1 = f32[4,4,64,1]{3,2,1,0:T(8,128)S(1)} collective-permute-done((f32[4,4,64,1]{3,2,1,0:T(8,128)S(1)}, f32[4,4,64,1]{3,2,1,0:T(8,128)S(1)}, u32[]{:S(2)}, u32[]{:S(2)}) %collective-permute-start.1) | collective-permute-done | bytes 4128 | tf_op jit(solution)/shard_map/ppermute | solution.py:22
  75.4 1.3 %fusion.17 = f32[4,4,64,512]{3,2,1,0:T(8,128)S(1)} fusion(f32[4,4,64,512]{3,2,1,0:T(8,128)S(1)} %get-tuple-element.9, f32[4,4,64,511]{3,2,1,0:T(8,128)S(1)} %bitcast.58, f32[4,4,64,1]{3,2,1,0:T(8,128)S(1)} %collective-permute-done.1, f32[4,4,64,512]{3,2,1,0:T(8,128)S(1)} %get-tuple-element.8, f32[4,4,63,512]{3,2,1,0:T(8,128)S(1)} %bitcast.59, ...), kind=kLoop, calls=%fused_computation.31 | loop fusion | flops 3145728 | bytes 10485760 | tf_op jit(solution)/shard_map/neg | solution.py:78
  76.8 0.9 %copy-done.17 = f32[4,64,512]{2,1,0:T(8,128)S(1)} copy-done((f32[4,64,512]{2,1,0:T(8,128)S(1)}, f32[4,64,512]{2,1,0:T(8,128)}, u32[]{:S(2)}) %copy-start.17) | copy-done | bytes 524312
  78.0 1.4 %copy-done.2 = f32[4,4,64,512]{3,2,1,0:T(8,128)S(1)} copy-done((f32[4,4,64,512]{3,2,1,0:T(8,128)S(1)}, f32[4,4,64,512]{3,2,1,0:T(8,128)}, u32[]{:S(2)}) %copy-start.2) | copy-done | bytes 2097176
  79.6 3.0 %multiply_add_fusion = (f32[4,4,64,512]{3,2,1,0:T(8,128)}, f32[4,4,64,512]{3,2,1,0:T(8,128)}) fusion(f32[4,4,64,512]{3,2,1,0:T(8,128)S(1)} %get-tuple-element.17, f32[4,4,64,512]{3,2,1,0:T(8,128)S(1)} %copy-done.2, f32[1,4,64,512]{3,2,1,0:T(8,128)S(1)} %copy-done.9, f32[1,4,64,512]{3,2,1,0:T(8,128)S(1)} %copy-done.11, f32[1,4,64,512]{3,2,1,0:T(8,128)S(1)} %copy-done.7, ...), kind=kLoop, calls=%fused_computation.38 | loop fusion | flops 6815744 | bytes 12058624 | tf_op jit(solution)/shard_map/add | solution.py:83
  (51 shorter events, 1.0 us)
Async XLA Ops:
  0.6 2.8 %copy-start.16 = (f32[4,4,64,512]{3,2,1,0:T(8,128)S(1)}, f32[4,4,64,512]{3,2,1,0:T(8,128)}, u32[]{:S(2)}) copy-start(f32[4,4,64,512]{3,2,1,0:T(8,128)} %param.6) | copy-start | bytes 6291460
  1.9 4.2 %copy-start.6 = (f32[1,4,64,512]{3,2,1,0:T(8,128)}, f32[1,4,64,512]{3,2,1,0:T(8,128)S(1)}, u32[]{:S(2)}) copy-start(f32[1,4,64,512]{3,2,1,0:T(8,128)S(1)} %convert_bitcast_fusion.2) | copy-start | bytes 1572868
  3.4 2.7 %copy-start.8 = (f32[1,4,64,512]{3,2,1,0:T(8,128)}, f32[1,4,64,512]{3,2,1,0:T(8,128)S(1)}, u32[]{:S(2)}) copy-start(f32[1,4,64,512]{3,2,1,0:T(8,128)S(1)} %get-tuple-element.18) | copy-start | bytes 1572868
  3.4 2.7 %copy-start.10 = (f32[1,4,64,512]{3,2,1,0:T(8,128)}, f32[1,4,64,512]{3,2,1,0:T(8,128)S(1)}, u32[]{:S(2)}) copy-start(f32[1,4,64,512]{3,2,1,0:T(8,128)S(1)} %get-tuple-element.19) | copy-start | bytes 1572868
  6.1 1.4 %copy-start.1 = (f32[4,4,64,512]{3,2,1,0:T(8,128)}, f32[4,4,64,512]{3,2,1,0:T(8,128)S(1)}, u32[]{:S(2)}) copy-start(f32[4,4,64,512]{3,2,1,0:T(8,128)S(1)} %get-tuple-element.16) | copy-start | bytes 6291460
  9.0 2.0 %copy-start.3 = (f32[8,4,64,512]{3,1,0,2:T(4,128)}, f32[8,4,64,512]{3,1,0,2:T(4,128)S(1)}, u32[]{:S(2)}) copy-start(f32[8,4,64,512]{3,1,0,2:T(4,128)S(1)} %copy_dynamic-update-slice_fusion) | copy-start | bytes 12582916
  9.0 10.8 %copy-start.12 = (s32[4,64,512]{2,1,0:T(8,128)S(1)}, s32[4,64,512]{2,1,0:T(8,128)}, u32[]{:S(2)}) copy-start(s32[4,64,512]{2,1,0:T(8,128)} %param.9) | copy-start | bytes 1572868
  9.0 10.8 %copy-start.14 = (s32[4,64,512]{2,1,0:T(8,128)S(1)}, s32[4,64,512]{2,1,0:T(8,128)}, u32[]{:S(2)}) copy-start(s32[4,64,512]{2,1,0:T(8,128)} %param.10) | copy-start | bytes 1572868
  9.0 12.9 %collective-permute-start.2 = (f32[8,4,512]{2,1,0:T(4,128)S(1)}, f32[8,4,512]{2,1,0:T(4,128)S(1)}, u32[]{:S(2)}, u32[]{:S(2)}) collective-permute-start(f32[8,4,512]{2,1,0:T(4,128)S(1)} %get-tuple-element.10), channel_id=1, source_target_pairs={{0,2},{2,0},{4,6},{6,4},{8,10},{10,8},{12,14},{14,12},{16,18},{18,... | collective-permute-start | bytes 196616 | tf_op jit(solution)/shard_map/ppermute | solution.py:17
  9.6 43.7 %collective-permute-start.6 = (f32[8,4,1,512]{3,1,0,2:T(4,128)S(1)}, f32[8,4,1,512]{3,1,0,2:T(4,128)S(1)}, u32[]{:S(2)}, u32[]{:S(2)}) collective-permute-start(f32[8,4,1,512]{3,1,0,2:T(4,128)S(1)} %get-tuple-element.11), channel_id=1, source_target_pairs={{1,0},{3,2},{5,4},{7,6},{9,8},{11,10},{13,12},{15,14},{17,16},{19,... | collective-permute-start | bytes 196616 | tf_op jit(solution)/shard_map/ppermute | solution.py:28
  13.9 33.3 %collective-permute-start = (f32[8,4,64,1]{2,0,3,1:T(8,128)S(1)}, f32[8,4,64,1]{2,0,3,1:T(8,128)S(1)}, u32[]{:S(2)}, u32[]{:S(2)}) collective-permute-start(f32[8,4,64,1]{2,0,3,1:T(8,128)S(1)} %copy.47), channel_id=1, source_target_pairs={{0,30},{2,0},{4,2},{6,4},{8,6},{10,8},{12,10},{14,12},{16,14},{18,... | collective-permute-start | bytes 24584 | tf_op jit(solution)/shard_map/ppermute | solution.py:22
  22.0 4.3 %collective-permute-start.3 = (f32[8,4,512]{2,1,0:T(4,128)S(1)}, f32[8,4,512]{2,1,0:T(4,128)S(1)}, u32[]{:S(2)}, u32[]{:S(2)}) collective-permute-start(f32[8,4,512]{2,1,0:T(4,128)S(1)} %collective-permute-done.2), channel_id=1, source_target_pairs={{0,4},{2,6},{4,0},{6,2},{8,12},{10,14},{12,8},{14,10},{16,20},{18,... | collective-permute-start | bytes 196616 | tf_op jit(solution)/shard_map/ppermute | solution.py:17
  26.2 21.4 %collective-permute-start.4 = (f32[8,4,512]{2,1,0:T(4,128)S(1)}, f32[8,4,512]{2,1,0:T(4,128)S(1)}, u32[]{:S(2)}, u32[]{:S(2)}) collective-permute-start(f32[8,4,512]{2,1,0:T(4,128)S(1)} %collective-permute-done.3), channel_id=1, source_target_pairs={{0,8},{2,10},{4,12},{6,14},{8,0},{10,2},{12,4},{14,6},{16,24},{18,... | collective-permute-start | bytes 196616 | tf_op jit(solution)/shard_map/ppermute | solution.py:17
  26.3 5.6 %copy-start.4 = (f32[8,4,64,512]{3,1,0,2:T(4,128)S(1)}, f32[8,4,64,512]{3,1,0,2:T(4,128)}, u32[]{:S(2)}) copy-start(f32[8,4,64,512]{3,1,0,2:T(4,128)} %copy-done.3) | copy-start | bytes 12582916
  36.1 6.7 %copy-start.5 = (f32[8,4,63,512]{3,1,0,2:T(4,128)S(1)}, f32[8,4,63,512]{3,1,0,2:T(4,128)}, u32[]{:S(2)}) copy-start(f32[8,4,63,512]{3,1,0,2:T(4,128)} %slice.110) | copy-start | bytes 12386308
  47.6 5.7 %copy-start.18 = (f32[8]{0:T(128)S(1)}, f32[8]{0:T(128)}, u32[]{:S(2)}) copy-start(f32[8]{0:T(128)} %constant.38.clone) | copy-start | bytes 100
  47.6 5.2 %collective-permute-start.5 = (f32[8,4,512]{2,1,0:T(4,128)S(1)}, f32[8,4,512]{2,1,0:T(4,128)S(1)}, u32[]{:S(2)}, u32[]{:S(2)}) collective-permute-start(f32[8,4,512]{2,1,0:T(4,128)S(1)} %collective-permute-done.4), channel_id=1, source_target_pairs={{0,16},{2,18},{4,20},{6,22},{8,24},{10,26},{12,28},{14,30},{16,0},... | collective-permute-start | bytes 196616 | tf_op jit(solution)/shard_map/ppermute | solution.py:17
  53.5 10.7 %copy-start = (f32[8,4,63,512]{3,2,1,0:T(8,128)S(1)}, f32[8,4,63,512]{3,2,1,0:T(8,128)}, u32[]{:S(2)}) copy-start(f32[8,4,63,512]{3,2,1,0:T(8,128)} %copy.52) | copy-start | bytes 12386308
  53.5 10.7 %copy-start.13 = (f32[4,64,512]{2,1,0:T(8,128)S(1)}, f32[4,64,512]{2,1,0:T(8,128)}, u32[]{:S(2)}) copy-start(f32[4,64,512]{2,1,0:T(8,128)} %reduce-window_subtract_fusion.1) | copy-start | bytes 1572868
  53.5 10.7 %copy-start.15 = (s32[4,64,512]{2,1,0:T(8,128)S(1)}, s32[4,64,512]{2,1,0:T(8,128)}, u32[]{:S(2)}) copy-start(s32[4,64,512]{2,1,0:T(8,128)} %param.10) | copy-start | bytes 1572868
  59.4 16.1 %collective-permute-start.7 = (f32[4,4,1,512]{3,2,1,0:T(1,128)S(1)}, f32[4,4,1,512]{3,2,1,0:T(1,128)S(1)}, u32[]{:S(2)}, u32[]{:S(2)}) collective-permute-start(f32[4,4,1,512]{3,2,1,0:T(1,128)S(1)} %slice.117), channel_id=1, source_target_pairs={{0,1},{2,3},{4,5},{6,7},{8,9},{10,11},{12,13},{14,15},{16,17},{18,... | collective-permute-start | bytes 98312 | tf_op jit(solution)/shard_map/ppermute | solution.py:28
  63.9 11.6 %collective-permute-start.1 = (f32[4,4,64,1]{3,2,1,0:T(8,128)S(1)}, f32[4,4,64,1]{3,2,1,0:T(8,128)S(1)}, u32[]{:S(2)}, u32[]{:S(2)}) collective-permute-start(f32[4,4,64,1]{3,2,1,0:T(8,128)S(1)} %slice.107), channel_id=1, source_target_pairs={{0,2},{2,4},{4,6},{6,8},{8,10},{10,12},{12,14},{14,16},{16,18},{18... | collective-permute-start | bytes 12296 | tf_op jit(solution)/shard_map/ppermute | solution.py:22
  76.7 1.0 %copy-start.17 = (f32[4,64,512]{2,1,0:T(8,128)S(1)}, f32[4,64,512]{2,1,0:T(8,128)}, u32[]{:S(2)}) copy-start(f32[4,64,512]{2,1,0:T(8,128)} %fusion.24) | copy-start | bytes 1572868
  76.7 1.3 %copy-start.11 = (f32[1,4,64,512]{3,2,1,0:T(8,128)S(1)}, f32[1,4,64,512]{3,2,1,0:T(8,128)}, u32[]{:S(2)}) copy-start(f32[1,4,64,512]{3,2,1,0:T(8,128)} %copy-done.10) | copy-start | bytes 1572868
  77.8 1.6 %copy-start.2 = (f32[4,4,64,512]{3,2,1,0:T(8,128)S(1)}, f32[4,4,64,512]{3,2,1,0:T(8,128)}, u32[]{:S(2)}) copy-start(f32[4,4,64,512]{3,2,1,0:T(8,128)} %copy-done.1) | copy-start | bytes 6291460
  77.8 1.7 %copy-start.7 = (f32[1,4,64,512]{3,2,1,0:T(8,128)S(1)}, f32[1,4,64,512]{3,2,1,0:T(8,128)}, u32[]{:S(2)}) copy-start(f32[1,4,64,512]{3,2,1,0:T(8,128)} %copy-done.6) | copy-start | bytes 1572868
  77.8 1.9 %copy-start.9 = (f32[1,4,64,512]{3,2,1,0:T(8,128)S(1)}, f32[1,4,64,512]{3,2,1,0:T(8,128)}, u32[]{:S(2)}) copy-start(f32[1,4,64,512]{3,2,1,0:T(8,128)} %copy-done.8) | copy-start | bytes 1572868
where the time goes:
time: 83 us; the launch traced here: 82.6 us
  local copies, waits for them, and re-layouts  30.6 us (37%)
  other arithmetic  22.2 us (27%)
  waiting for transfers between devices  15.5 us (19%)
  starting transfers between devices  13.4 us (16%)
  between operations  1 us (1%)
    ppermute x2, waiting for transfers between devices, passed_along(): lax.ppermute(x, axis, [(i, (i + by) % length) for i in range(length)])  11 us
    slice x2, local copies, waits for them, and re-layouts, shards(): east = jnp.concatenate([both[:, :, :, 1:], east_col], 3)  11 us
    slice x2, local copies, waits for them, and re-layouts, shards(): north = jnp.concatenate([both[:, :, 1:, :], north_row[:, :, None, :]], 2)  9.97 us
    ppermute x2, starting transfers between devices, passed_along(): lax.ppermute(x, axis, [(i, (i + by) % length) for i in range(length)])  6.1 us
    sub x1, other arithmetic, face_flux(): advect_coef * speed * (here[:4] + ahead[:4]) * 0.5  5.84 us
    ppermute x2, starting transfers between devices, passed_along_2(): return lax.ppermute(x, axis, pairs)  5.68 us
    ppermute x4, waiting for transfers between devices, from_partner(): lax.ppermute(x, axis, [(i, i ^ 1 << stride) for i in range(lax.axis_size(...  4.48 us
    another operation x3, other arithmetic, pressure(): return jnp.cumsum(density, axis=0) - 0.5 * density  4.2 us
  transfers between devices with their start and end apart: 8, of which 3 were waited for; matrix products, arithmetic and copies ran while one was open for 38% of the time, Pallas kernels for 0%

commit v1 on v0

v1 whole, which is shorter than its diff:
```python
import functools

import jax
import jax.numpy as jnp
from jax import lax
from jax.experimental import pallas as pl
from jax.experimental.pallas import tpu as pltpu
from jax.sharding import PartitionSpec as P

advect_coef = 0.5
diffuse_coef = 0.25
twice_step = 0.5
gravity = 0.5
coriolis = 0.5
thermal = 0.2
haline = 0.15
asselin = 0.1

LANES = 128
SUBS = 8
FIELDS = 4
LEVELS = 4
ROWS = FIELDS * LEVELS
VMEM_LIMIT = 24 * 1024 * 1024

speed_coef = advect_coef * 0.5
ANY = pl.BlockSpec(memory_space=pl.ANY)
VMEM = pl.BlockSpec(memory_space=pltpu.VMEM)


def mask_of(field):
    return max(field - 1, 0)


def lane_ids(shape):
    return lax.broadcasted_iota(jnp.int32, shape, len(shape) - 1)


def row_ids(shape):
    return lax.broadcasted_iota(jnp.int32, shape, len(shape) - 2)


def halved(x):
    half = x.shape[0] // 2
    return jnp.where(lane_ids((half, LANES)) < LANES // 2, x[:half], pltpu.roll(x[half:], LANES // 2, 1))


def edges_kernel(
    n_lat,
    earlier, present, scalar_flags, east_flags, north_flags,
    pay_a, pay_b, pay_west, pay_east, coef_north, coef_south, coef_west, coef_east,
    col_state, col_flag, row_state, row_flag, sems,
):
    height, width = present.shape[2], present.shape[3]
    lat = lax.axis_index("lat")
    flags = (scalar_flags, east_flags, north_flags)
    copies = []
    for side in range(2):
        rows = pl.ds(0 if side == 0 else height - SUBS, SUBS)
        for t, state in enumerate((present, earlier)):
            copies.append((state.at[:, :, rows, :], row_state.at[side, t]))
        for t, flag in enumerate(flags):
            copies.append((flag.at[:, rows, :], row_flag.at[side, t]))
    for side in range(2):
        cols = pl.ds(0 if side == 0 else width - LANES, LANES)
        for t, state in enumerate((present, earlier)):
            copies.append((state.at[:, :, :, cols], col_state.at[side, t]))
        for t, flag in enumerate(flags):
            copies.append((flag.at[:, :, cols], col_flag.at[side, t]))
    copies = [
        pltpu.make_async_copy(src, dst, sems.at[i]) for i, (src, dst) in enumerate(copies)
    ]
    for copy in copies:
        copy.start()
    for copy in copies[:10]:
        copy.wait()

    sub = row_ids((SUBS, LANES))
    n_tiles = width // LANES

    def row_pack(side, at, j):
        line = pl.ds(at, 1)
        cols = pl.ds(j * LANES, LANES)

        def gather(rows):
            packed = jnp.broadcast_to(rows[0], (SUBS, LANES))
            for k in range(1, SUBS):
                packed = jnp.where(sub == k, jnp.broadcast_to(rows[k], (SUBS, LANES)), packed)
            return packed

        def flag_row(t, l):
            return row_flag[side, t, l, line, cols].astype(jnp.float32)

        fm = [
            gather([flag_row(mask_of(f), l) for f in (2 * h, 2 * h + 1) for l in range(LEVELS)])
            for h in range(2)
        ]
        cur, bef = (
            [
                fm[h]
                * gather([row_state[side, t, f, l, line, cols] for f in (2 * h, 2 * h + 1) for l in range(LEVELS)])
                for h in range(2)
            ]
            for t in range(2)
        )
        return fm, cur, bef

    lane = lane_ids((SUBS, LANES))
    back = LANES - 1 - lane
    even = lat % 2 == 0
    is_top = lat == n_lat - 1
    for j in range(n_tiles):
        cols = pl.ds(j * LANES, LANES)
        fm, cur, bef = row_pack(1, SUBS - 1, j)
        low_v = pltpu.roll(cur[1], 4, 0)
        s = speed_coef * jnp.where(sub < 4, low_v, cur[1])
        m = diffuse_coef * jnp.where(sub < 4, pltpu.roll(fm[1], 4, 0), fm[1])
        g = [s * cur[h] + m * bef[h] for h in range(2)]
        for h in range(2):
            at = pl.ds(h * SUBS, SUBS)
            coef_north[at, cols] = -twice_step * fm[h] * s
            coef_north[pl.ds(ROWS + h * SUBS, SUBS), cols] = twice_step * fm[h] * m
        coef_north[pl.ds(2 * ROWS, SUBS), cols] = jnp.where(sub < 4, 0.0, -twice_step * gravity * fm[1])

        fm_s, cur_s, bef_s = row_pack(0, 0, j)
        for h in range(2):
            at = pl.ds(h * SUBS, SUBS)
            coef_south[at, cols] = twice_step * fm_s[h]
            coef_south[pl.ds(ROWS + h * SUBS, SUBS), cols] = twice_step * cur_s[h]
            coef_south[pl.ds(2 * ROWS + h * SUBS, SUBS), cols] = -twice_step * bef_s[h]

        north_going = g + [s, m]
        south_going = cur_s + bef_s
        for q in range(4):
            at = pl.ds(q * SUBS, SUBS)
            pay_a[at, cols] = jnp.where(even, north_going[q], south_going[q])

        @pl.when(jnp.logical_not(is_top))
        def _():
            for q in range(4):
                below = jnp.where(lat == 0, 0.0, south_going[q])
                pay_b[pl.ds((4 * j + q) * SUBS, SUBS), :] = jnp.where(even, below, north_going[q])

        @pl.when(is_top)
        def _():
            for q, x in enumerate(cur + bef):
                mirrored = pl.ds((4 * (n_tiles - 1 - j) + q) * SUBS, SUBS)
                turned = jnp.take_along_axis(x, back, axis=1)
                pay_b[mirrored, :] = turned if q % 2 == 0 else -turned

    for copy in copies[10:]:
        copy.wait()

    lane = lane_ids((height, LANES))
    def col_pack(side, at):
        def column(x):
            return jnp.broadcast_to(x[:, at : at + 1], (height, LANES))

        def flag_col(t, l):
            return column(col_flag[side, t, l, :, :].astype(jnp.float32))

        masks = [[flag_col(t, l) for l in range(LEVELS)] for t in range(3)]
        base = lane & 15
        fm = masks[2][LEVELS - 1]
        for f in range(FIELDS):
            for l in range(LEVELS):
                if f * LEVELS + l < ROWS - 1:
                    fm = jnp.where(base == f * LEVELS + l, masks[mask_of(f)][l], fm)
        both = jnp.zeros((height, LANES), jnp.float32)
        u = []
        for t in range(2):
            for f in range(FIELDS):
                for l in range(LEVELS):
                    x = column(col_state[side, t, f, l, :, :])
                    if t == 0 and f == 2:
                        u.append(x)
                    both = jnp.where(lane == t * ROWS + f * LEVELS + l, x, both)
        return masks[1], fm, both * fm, u

    level = lane & 3
    _, fm, both, _ = col_pack(0, 0)
    rho = jnp.where(lane < LEVELS, haline * pltpu.roll(both, LANES - LEVELS, 1) - thermal * both, 0.0)
    total = rho + pltpu.roll(rho, 1, 1)
    total = total + pltpu.roll(total, 2, 1)
    pres = jnp.where(lane < LEVELS, total - 0.5 * rho, 0.0)
    going_west = both + pltpu.roll(pres, 2 * ROWS + 2 * LEVELS, 1)
    moved = pltpu.roll(both, ROWS, 1)
    coef_west[...] = twice_step * jnp.where(lane < ROWS, fm, jnp.where(lane < 2 * ROWS, moved, -moved))
    mu, fm, both, u = col_pack(1, LANES - 1)
    m, s = mu[LEVELS - 1], u[LEVELS - 1]
    for l in range(LEVELS - 1):
        m = jnp.where(level == l, mu[l], m)
        s = jnp.where(level == l, u[l], s)
    s = speed_coef * s * m
    dm = diffuse_coef * m
    own = both * jnp.where(lane < ROWS, s, dm)
    g = own + pltpu.roll(own, LANES - ROWS, 1)
    going_east = jnp.where(lane < ROWS, g, jnp.where(lane < 2 * ROWS, s, dm))
    pay_west[...] = halved(going_west)
    pay_east[...] = halved(going_east)
    face = jnp.where(lane < ROWS, -twice_step * s, twice_step * dm) * fm
    in_pres = (lane >= 2 * ROWS + 2 * LEVELS) & (lane < 2 * ROWS + 3 * LEVELS)
    coef_east[...] = jnp.where(
        lane < 2 * ROWS, face, jnp.where(in_pres, -twice_step * gravity * m, 0.0)
    )


def inner_kernel(
    total_rows,
    raw_bef, raw_cur, scalar_flags, east_flags, north_flags,
    after_v, filtered_v,
    cur_v, bef_v, pres_v, flux_v,
):
    height, width = raw_cur.shape[2], raw_cur.shape[3]
    n_chunks, n_tiles = height // SUBS, width // LANES
    lat = lax.axis_index("lat")
    flags = (scalar_flags, east_flags, north_flags)

    zero = jnp.zeros((SUBS, LANES), jnp.float32)
    lane = lane_ids((SUBS, LANES))
    sub = row_ids((SUBS, LANES))
    first_lane, last_lane = lane == 0, lane == LANES - 1
    tiles = [pl.ds(j * LANES, LANES) for j in range(n_tiles)]
    for l in range(LEVELS):
        for j in range(n_tiles):
            pres_v[l, j, pl.ds(height, SUBS), :] = zero
            for f in range(FIELDS):
                cur_v[f, l, j, pl.ds(height, SUBS), :] = zero
                bef_v[f, l, j, pl.ds(height, SUBS), :] = zero
                flux_v[f, l, j, pl.ds(0, SUBS), :] = zero

    def masked(c):
        rows = pl.ds(pl.multiple_of(c * SUBS, SUBS), SUBS)
        puts = []
        for j, cols in enumerate(tiles):
            total = zero
            for l in range(LEVELS):
                masks = [flags[t][l, rows, cols].astype(jnp.float32) for t in range(3)]
                cur = [raw_cur[f, l, rows, cols] * masks[mask_of(f)] for f in range(FIELDS)]
                rho = haline * cur[1] - thermal * cur[0]
                total = total + rho
                puts.append((pres_v, (l, j, rows), total - 0.5 * rho))
                for f in range(FIELDS):
                    puts.append((cur_v, (f, l, j, rows), cur[f]))
                    puts.append((bef_v, (f, l, j, rows), raw_bef[f, l, rows, cols] * masks[mask_of(f)]))
        return puts

    def store(puts):
        for ref, at, value in puts:
            ref[at] = value

    def east_of(x):
        beyond = x[1:] + [zero]
        return [pltpu.roll(jnp.where(first_lane, b, a), LANES - 1, 1) for a, b in zip(x, beyond)]

    def west_of(x):
        beyond = [zero] + x[:-1]
        return [pltpu.roll(jnp.where(last_lane, b, a), 1, 1) for a, b in zip(x, beyond)]

    def each(op, *xs):
        return [op(*x) for x in zip(*xs)]

    def face_flux(s, m, x, x_next, y, y_next):
        return each(lambda s, m, x, xn, y, yn: s * (x + xn) - m * (yn - y), s, m, x, x_next, y, y_next)

    def at(ref, r):
        return [ref[j, r, :] for j in range(n_tiles)]

    half = twice_step

    def north_fluxes(c):
        rows = pl.ds(pl.multiple_of(c * SUBS, SUBS), SUBS)
        shifted = pl.ds(c * SUBS + 1, SUBS)
        puts = []
        for l in range(LEVELS):
            s_n = [half * speed_coef * x for x in at(cur_v.at[3, l], rows)]
            m_n = [half * diffuse_coef * flags[2][l, rows, cols].astype(jnp.float32) for cols in tiles]
            for f in range(FIELDS):
                flux = face_flux(
                    s_n, m_n,
                    at(cur_v.at[f, l], rows), at(cur_v.at[f, l], shifted),
                    at(bef_v.at[f, l], rows), at(bef_v.at[f, l], shifted),
                )
                for j, x in enumerate(flux):
                    puts.append((flux_v, (f, l, j, pl.ds(pl.multiple_of((c + 1) * SUBS, SUBS), SUBS)), x))
        return puts

    def stepped(c):
        rows = pl.ds(pl.multiple_of(c * SUBS, SUBS), SUBS)
        shifted = pl.ds(c * SUBS + 1, SUBS)
        own_face = pl.ds(pl.multiple_of((c + 1) * SUBS, SUBS), SUBS)
        south_face = pl.ds((c + 1) * SUBS - 1, SUBS)
        index = (lat * height + c * SUBS + sub).astype(jnp.float32)
        cor = half * coriolis * (2.0 * (index + 0.5) / total_rows - 1.0)
        puts = []
        for l in range(LEVELS):
            masks = [[flags[t][l, rows, cols].astype(jnp.float32) for cols in tiles] for t in range(3)]
            cur = [at(cur_v.at[f, l], rows) for f in range(FIELDS)]
            bef = [at(bef_v.at[f, l], rows) for f in range(FIELDS)]
            pres = at(pres_v.at[l], rows)
            slope_e = each(lambda m, e, p: (half * gravity) * m * (e - p), masks[1], east_of(pres), pres)
            slope_n = each(lambda m, n, p: (half * gravity) * m * (n - p), masks[2], at(pres_v.at[l], shifted), pres)
            s_e, m_e = [half * speed_coef * x for x in cur[2]], [half * diffuse_coef * x for x in masks[1]]
            for f in range(FIELDS):
                flux_e = face_flux(s_e, m_e, cur[f], east_of(cur[f]), bef[f], east_of(bef[f]))
                flux_n = at(flux_v.at[f, l], own_face)
                flux_s = at(flux_v.at[f, l], south_face)
                tend = each(lambda w, e, s, n: (w - e) + (s - n), west_of(flux_e), flux_e, flux_s, flux_n)
                if f == 2:
                    tend = each(lambda t, v, g: t + (cor * v - g), tend, cur[3], slope_e)
                elif f == 3:
                    tend = each(lambda t, u, g: t - (cor * u + g), tend, cur[2], slope_n)
                new = each(lambda b, t, m: (b + t) * m, bef[f], tend, masks[mask_of(f)])
                mid = each(lambda c, b, n: (1.0 - 2.0 * asselin) * c + asselin * (b + n), cur[f], bef[f], new)
                for cols, a, x in zip(tiles, new, mid):
                    puts.append((after_v, (f, l, rows, cols), a))
                    puts.append((filtered_v, (f, l, rows, cols), x))
        return puts

    for c in range(2):
        store(masked(c))

    def chunk(c, carry):
        ahead = masked(jnp.minimum(c + 2, n_chunks - 1))
        faces = north_fluxes(c)
        store(ahead)
        store(faces)
        store(stepped(c))

        return carry

    lax.fori_loop(0, n_chunks, chunk, 0)


def rim_kernel(
    got_a, got_b, got_east, got_west, coef_north, coef_south, coef_west, coef_east,
    after_v, filtered_v,
    after, filtered, after_w, filtered_w,
    add_rows, add_cols, sems,
):
    height, width = after.shape[2], after.shape[3]
    n_chunks, n_tiles = height // SUBS, width // LANES
    lane = lane_ids((SUBS, LANES))
    sub = row_ids((SUBS, LANES))
    even = lax.axis_index("lat") % 2 == 0

    def out(i, rows, cols):
        copies = [
            pltpu.make_async_copy(s.at[:, :, rows, cols], d.at[:, :, rows, cols], sems.at[i, q])
            for q, (s, d) in enumerate(((after_w, after), (filtered_w, filtered)))
        ]
        for copy in copies:
            copy.start()
        return copies

    middle = pl.ds(SUBS, height - 2 * SUBS)
    pending = out(4, middle, pl.ds(LANES, width - 2 * LANES))

    for j in range(n_tiles):
        cols = pl.ds(j * LANES, LANES)
        got = [(got_a[pl.ds(q * SUBS, SUBS), cols], got_b[pl.ds((4 * j + q) * SUBS, SUBS), :]) for q in range(4)]
        north = [jnp.where(even, a, b) for a, b in got]
        south = [jnp.where(even, b, a) for a, b in got]

        def coef(ref, q):
            return ref[pl.ds(q * SUBS, SUBS), cols]

        rho = jnp.where(sub < LEVELS, haline * pltpu.roll(north[0], LEVELS, 0) - thermal * north[0], 0.0)
        total = rho + pltpu.roll(rho, 1, 0)
        total = total + pltpu.roll(total, 2, 0)
        pres = pltpu.roll(total - 0.5 * rho, LEVELS, 0)
        for h in range(2):
            at = pl.ds(h * SUBS, SUBS)
            up = coef(coef_north, h) * north[h] + coef(coef_north, 2 + h) * north[2 + h]
            if h == 1:
                up = up + coef(coef_north, 4) * pres
            add_rows[1, at, cols] = up
            add_rows[0, at, cols] = (
                coef(coef_south, h) * south[h]
                + coef(coef_south, 2 + h) * south[2]
                + coef(coef_south, 4 + h) * south[3]
            )

    def apply(f, l, rows, j, extra):
        cols = pl.ds(j * LANES, LANES)
        after_w[f, l, rows, cols] = after_v[f, l, rows, cols] + extra
        filtered_w[f, l, rows, cols] = filtered_v[f, l, rows, cols] + asselin * extra

    for side, (got, coef) in enumerate(((got_west[...], coef_west), (got_east[...], coef_east))):
        for part in range(2):
            rows = pl.ds(part * (height // 2), height // 2)
            x = got if part == 0 else pltpu.roll(got, LANES // 2, 1)
            x = x * coef[rows, :]
            add_cols[side, rows, :] = (
                x + pltpu.roll(x, LANES - ROWS, 1) + pltpu.roll(x, LANES - 2 * ROWS, 1)
            )

    def edge_cols(c):
        rows = pl.ds(pl.multiple_of(c * SUBS, SUBS), SUBS)
        return rows, add_cols[0, rows, :], add_cols[1, rows, :]

    def put(value, k, at):
        return jnp.where(lane == at, jnp.broadcast_to(value[:, k : k + 1], (SUBS, LANES)), 0.0)

    def row_chunk(c, side, line):
        rows, west, east = edge_cols(c)
        for f in range(FIELDS):
            for l in range(LEVELS):
                k = f * LEVELS + l
                for j in range(n_tiles):
                    row = add_rows[side, pl.ds(k, 1), pl.ds(j * LANES, LANES)]
                    extra = jnp.where(sub == line, jnp.broadcast_to(row, (SUBS, LANES)), 0.0)
                    if j == 0:
                        extra = extra + put(west, k, 0)
                    if j == n_tiles - 1:
                        extra = extra + put(east, k, LANES - 1)
                    apply(f, l, rows, j, extra)

    row_chunk(0, 0, 0)
    pending += out(0, pl.ds(0, SUBS), pl.ds(0, width))
    row_chunk(n_chunks - 1, 1, SUBS - 1)
    pending += out(1, pl.ds(height - SUBS, SUBS), pl.ds(0, width))

    def side_chunk(c, carry):
        rows, west, east = edge_cols(c)
        for f in range(FIELDS):
            for l in range(LEVELS):
                k = f * LEVELS + l
                apply(f, l, rows, 0, put(west, k, 0))
                apply(f, l, rows, n_tiles - 1, put(east, k, LANES - 1))
        return carry

    lax.fori_loop(1, n_chunks - 1, side_chunk, 0)
    pending += out(2, middle, pl.ds(0, LANES))
    pending += out(3, middle, pl.ds(width - LANES, LANES))
    for copy in pending:
        copy.wait()


def shards(n_lat, earlier_state, present_state, scalar_wet_flags, eastside_wet_flags, northside_wet_flags):
    args = (earlier_state, present_state, scalar_wet_flags, eastside_wet_flags, northside_wet_flags)
    height, width = present_state.shape[2:]
    n_lon = lax.axis_size("lon")
    f32 = jnp.float32
    params = pltpu.CompilerParams(vmem_limit_bytes=VMEM_LIMIT)
    state = (FIELDS, LEVELS, height, width)
    apart = (LEVELS, width // LANES, height + SUBS, LANES)

    def vmem(*shape):
        return pltpu.VMEM(shape, f32)

    edges = pl.pallas_call(
        functools.partial(edges_kernel, n_lat),
        out_shape=[
            vmem(2 * ROWS, width), vmem(2 * ROWS * (width // LANES), LANES),
            vmem(height // 2, LANES), vmem(height // 2, LANES),
            vmem(2 * ROWS + SUBS, width), vmem(3 * ROWS, width), vmem(height, LANES), vmem(height, LANES),
        ],
        in_specs=[ANY] * 5,
        out_specs=[VMEM] * 8,
        scratch_shapes=[
            pltpu.VMEM((2, 2, FIELDS, LEVELS, height, LANES), f32),
            pltpu.VMEM((2, 3, LEVELS, height, LANES), jnp.int32),
            pltpu.VMEM((2, 2, FIELDS, LEVELS, SUBS, width), f32),
            pltpu.VMEM((2, 3, LEVELS, SUBS, width), jnp.int32),
            pltpu.SemaphoreType.DMA((20,)),
        ],
        compiler_params=params,
        cost_estimate=pl.CostEstimate(flops=500_000, bytes_accessed=3_600_000, transcendentals=0),
        name="edges",
    )(*[pltpu.with_memory_space_constraint(x, pltpu.HBM) for x in args])
    pay_a, pay_b, pay_west, pay_east, *coefs = edges

    def device(lon, lat):
        return lon * n_lat + lat

    lons, lats, top = range(n_lon), range(n_lat), n_lat - 1
    pairs_a = [(device(lon, lat), device(lon, lat ^ 1)) for lon in lons for lat in lats]
    pairs_b = [
        (
            device(lon, lat),
            device(n_lon - 1 - lon, lat) if lat in (0, top) else device(lon, lat + 1 if lat % 2 else lat - 1),
        )
        for lon in lons
        for lat in lats
    ]
    got_b = lax.ppermute(pay_b, ("lon", "lat"), pairs_b)
    got_a = lax.ppermute(pay_a, ("lon", "lat"), pairs_a)
    got_east = lax.ppermute(pay_west, "lon", [(i, (i - 1) % n_lon) for i in lons])
    got_west = lax.ppermute(pay_east, "lon", [(i, (i + 1) % n_lon) for i in lons])

    after_v, filtered_v = pl.pallas_call(
        functools.partial(inner_kernel, height * n_lat),
        out_shape=[vmem(*state), vmem(*state)],
        in_specs=[VMEM] * 5,
        out_specs=[VMEM, VMEM],
        scratch_shapes=[
            pltpu.VMEM((FIELDS, *apart), f32),
            pltpu.VMEM((FIELDS, *apart), f32),
            pltpu.VMEM(apart, f32),
            pltpu.VMEM((FIELDS, *apart), f32),
        ],
        compiler_params=params,
        cost_estimate=pl.CostEstimate(flops=20_000_000, bytes_accessed=9_000_000, transcendentals=0),
        name="inner",
    )(*[pltpu.with_memory_space_constraint(x, pltpu.VMEM) for x in args])

    def in_vmem(x):
        return pltpu.with_memory_space_constraint(x, pltpu.VMEM)

    fixed = [in_vmem(x) for x in (got_a, got_b, got_east, got_west, *coefs, after_v, filtered_v)]
    after, filtered, _, _ = pl.pallas_call(
        rim_kernel,
        out_shape=[pltpu.HBM(state, f32), pltpu.HBM(state, f32), vmem(*state), vmem(*state)],
        in_specs=[VMEM] * 10,
        out_specs=[ANY, ANY, VMEM, VMEM],
        scratch_shapes=[
            pltpu.VMEM((2, ROWS, width), f32),
            pltpu.VMEM((2, height, LANES), f32),
            pltpu.SemaphoreType.DMA((5, 2)),
        ],
        input_output_aliases={8: 2, 9: 3},
        compiler_params=params,
        cost_estimate=pl.CostEstimate(flops=500_000, bytes_accessed=3_000_000, transcendentals=0),
        name="rim",
    )(*fixed)
    return after, filtered


def solution(mesh):
    placed = (
        P(None, None, "lat", "lon"),
        P(None, None, "lat", "lon"),
        P(None, "lat", "lon"),
        P(None, "lat", "lon"),
        P(None, "lat", "lon"),
    )
    return jax.shard_map(
        functools.partial(shards, mesh.shape["lat"]),
        mesh=mesh,
        in_specs=placed,
        out_specs=(P(None, None, "lat", "lon"), P(None, None, "lat", "lon")),
        check_vma=False,
    )
```

time: 83 us -> 23.5 us (0.28)
  the two profiles are of different devices: /device:TPU:0 before, /device:TPU:1 now
where the time goes in v1:
time: 23.5 us; the launch traced here: 23.3 us
  Pallas kernels  13.6 us (58%)
  starting transfers between devices  8.97 us (38%)
  between operations  0.73 us (3%)
    pallas_call x1, Pallas kernels, shards(): pl.pallas_call(functools.partial(inner_kernel, height * n_lat), out_shape...  6.98 us
    ppermute x1, starting transfers between devices, shards(): got_b = lax.ppermute(pay_b, ('lon', 'lat'), pairs_b)  5.09 us
    pallas_call x1, Pallas kernels, shards(): pl.pallas_call(functools.partial(edges_kernel, n_lat), out_shape=[vmem(2...  3.8 us
    pallas_call x1, Pallas kernels, shards(): pl.pallas_call(rim_kernel, out_shape=[pltpu.HBM(state, f32), pltpu.HBM(st...  2.79 us
    ppermute x1, starting transfers between devices, shards(): got_a = lax.ppermute(pay_a, ('lon', 'lat'), pairs_a)  2.13 us
    ppermute x1, starting transfers between devices, shards(): lax.ppermute(pay_east, 'lon', [(i, (i + 1) % n_lon) for i in lons])  1.74 us
  transfers between devices with their start and end apart: 4, of which 0 were waited for; matrix products, arithmetic and copies ran while one was open for 0% of the time, Pallas kernels for 30%

profile of v1, /device:TPU:1, one launch (start us, length us, event | category | flops | bytes accessed | tf_op | source)
XLA Modules:
  0.0 23.3 jit_solution(15082776373919370580)
XLA Ops:
  0.6 0.0 copy-start.4
  0.6 0.0 copy-start.3
  0.7 0.0 copy-start.2
  0.7 0.0 copy-start.1
  0.7 0.0 copy-start
  0.7 3.8 %edges.1 = (f32[32,512]{1,0:T(8,128)S(1)}, f32[128,128]{1,0:T(8,128)S(1)}, f32[32,128]{1,0:T(8,128)S(1)}, f32[32,128]{1,0:T(8,128)S(1)}, f32[40,512]{1,0:T(8,128...) custom-call(f32[4,4,64,512]{3,2,1,0:T(8,128)} %raw_bef.1, f32[4,4,64,512]{3,2,1,0:T(8,128)} %raw_cur.1, ...), custom_call_target="tpu_custom_call" | custom-call | flops 500000 | bytes 3600000 | tf_op jit(solution)/shard_map/edges/pallas_call | solution.py:452
  4.5 2.1 %collective-permute-start = (f32[32,512]{1,0:T(8,128)S(1)}, f32[32,512]{1,0:T(8,128)S(1)}, u32[]{:S(2)}, u32[]{:S(2)}) collective-permute-start(f32[32,512]{1,0:T(8,128)S(1)} %get-tuple-element.14), channel_id=1, source_target_pairs={{0,1},{1,0},{2,3},{3,2},{4,5},{5,4},{6,7},{7,6},{8,9},{9,8},{10,11... | collective-permute-start | bytes 196616 | tf_op jit(solution)/shard_map/ppermute | solution.py:488
  6.6 5.1 %collective-permute-start.1 = (f32[128,128]{1,0:T(8,128)S(1)}, f32[128,128]{1,0:T(8,128)S(1)}, u32[]{:S(2)}, u32[]{:S(2)}) collective-permute-start(f32[128,128]{1,0:T(8,128)S(1)} %get-tuple-element.15), channel_id=1, source_target_pairs={{0,30},{1,31},{2,28},{3,29},{4,26},{5,27},{6,24},{7,25},{8,22},{9,... | collective-permute-start | bytes 196616 | tf_op jit(solution)/shard_map/ppermute | solution.py:487
  11.7 0.0 collective-permute-start.2
  11.7 1.7 %collective-permute-start.3 = (f32[32,128]{1,0:T(8,128)S(1)}, f32[32,128]{1,0:T(8,128)S(1)}, u32[]{:S(2)}, u32[]{:S(2)}) collective-permute-start(f32[32,128]{1,0:T(8,128)S(1)} %get-tuple-element.17), channel_id=1, source_target_pairs={{0,2},{2,4},{4,6},{6,8},{8,10},{10,12},{12,14},{14,16},{16,18},{18... | collective-permute-start | bytes 49160 | tf_op jit(solution)/shard_map/ppermute | solution.py:490
  13.5 0.0 copy-done.4
  13.5 0.0 copy-done.3
  13.5 0.0 copy-done.2
  13.5 0.0 copy-done.1
  13.5 0.0 copy-done
  13.5 7.0 %inner.1 = (f32[4,4,64,512]{3,2,1,0:T(8,128)S(1)}, f32[4,4,64,512]{3,2,1,0:T(8,128)S(1)}) custom-call(f32[4,4,64,512]{3,2,1,0:T(8,128)S(1)} %copy-done, f32[4,4,64,512]{3,2,1,0:T(8,128)S(1)} %copy-done.1, s32[4,64,512]{2,1,0:T(8,128)S(1)} %copy-done.2, s32[4,64,512]{2,1,0:T(8,128)S(1)} %copy-done.3, s32[4,64,512]{2,1,0:T(8,128)S(1)} %copy-done.4), custom_call_target="tpu_custom_call" | custom-call | flops 20000000 | bytes 9000000 | tf_op jit(solution)/shard_map/inner/pallas_call | solution.py:492
  20.5 0.0 collective-permute-done.2.got_east
  20.5 0.0 collective-permute-done.3.got_west
  20.5 0.0 collective-permute-done.got_a
  20.5 0.0 collective-permute-done.1.got_b
  20.5 2.8 %rim.1 = (f32[4,4,64,512]{3,2,1,0:T(8,128)}, f32[4,4,64,512]{3,2,1,0:T(8,128)}, f32[4,4,64,512]{3,2,1,0:T(8,128)S(1)}, f32[4,4,64,512]{3,2,1,0:T(8,128)S(1)}) custom-call(f32[32,512]{1,0:T(8,128)S(1)} %collective-permute-done.got_a, f32[128,128]{1,0:T(8,128)S(1)} %collective-permute-done.1.got_b, ...), custom_call_target="tpu_custom_call", output_to_operand_aliasing={{2}: (8, {}), {3}: (9, {})} | custom-call | flops 500000 | bytes 3000000 | tf_op jit(solution)/shard_map/rim/pallas_call | solution.py:512
Async XLA Ops:
  0.6 12.8 %copy-start.4 = (s32[4,64,512]{2,1,0:T(8,128)S(1)}, s32[4,64,512]{2,1,0:T(8,128)}, u32[]{:S(2)}) copy-start(s32[4,64,512]{2,1,0:T(8,128)} %north_flags.3) | copy-start | bytes 1572868
  0.6 12.8 %copy-start.3 = (s32[4,64,512]{2,1,0:T(8,128)S(1)}, s32[4,64,512]{2,1,0:T(8,128)}, u32[]{:S(2)}) copy-start(s32[4,64,512]{2,1,0:T(8,128)} %east_flags.3) | copy-start | bytes 1572868
  0.7 12.8 %copy-start.2 = (s32[4,64,512]{2,1,0:T(8,128)S(1)}, s32[4,64,512]{2,1,0:T(8,128)}, u32[]{:S(2)}) copy-start(s32[4,64,512]{2,1,0:T(8,128)} %scalar_flags.3) | copy-start | bytes 1572868
  0.7 12.8 %copy-start.1 = (f32[4,4,64,512]{3,2,1,0:T(8,128)S(1)}, f32[4,4,64,512]{3,2,1,0:T(8,128)}, u32[]{:S(2)}) copy-start(f32[4,4,64,512]{3,2,1,0:T(8,128)} %raw_cur.1) | copy-start | bytes 6291460
  0.7 12.8 %copy-start = (f32[4,4,64,512]{3,2,1,0:T(8,128)S(1)}, f32[4,4,64,512]{3,2,1,0:T(8,128)}, u32[]{:S(2)}) copy-start(f32[4,4,64,512]{3,2,1,0:T(8,128)} %raw_bef.1) | copy-start | bytes 6291460
  4.5 16.0 %collective-permute-start = (f32[32,512]{1,0:T(8,128)S(1)}, f32[32,512]{1,0:T(8,128)S(1)}, u32[]{:S(2)}, u32[]{:S(2)}) collective-permute-start(f32[32,512]{1,0:T(8,128)S(1)} %get-tuple-element.14), channel_id=1, source_target_pairs={{0,1},{1,0},{2,3},{3,2},{4,5},{5,4},{6,7},{7,6},{8,9},{9,8},{10,11... | collective-permute-start | bytes 196616 | tf_op jit(solution)/shard_map/ppermute | solution.py:488
  6.6 13.9 %collective-permute-start.1 = (f32[128,128]{1,0:T(8,128)S(1)}, f32[128,128]{1,0:T(8,128)S(1)}, u32[]{:S(2)}, u32[]{:S(2)}) collective-permute-start(f32[128,128]{1,0:T(8,128)S(1)} %get-tuple-element.15), channel_id=1, source_target_pairs={{0,30},{1,31},{2,28},{3,29},{4,26},{5,27},{6,24},{7,25},{8,22},{9,... | collective-permute-start | bytes 196616 | tf_op jit(solution)/shard_map/ppermute | solution.py:487
  11.7 8.8 %collective-permute-start.2 = (f32[32,128]{1,0:T(8,128)S(1)}, f32[32,128]{1,0:T(8,128)S(1)}, u32[]{:S(2)}, u32[]{:S(2)}) collective-permute-start(f32[32,128]{1,0:T(8,128)S(1)} %get-tuple-element.16), channel_id=1, source_target_pairs={{0,30},{2,0},{4,2},{6,4},{8,6},{10,8},{12,10},{14,12},{16,14},{18,... | collective-permute-start | bytes 49160 | tf_op jit(solution)/shard_map/ppermute | solution.py:489
  11.7 8.8 %collective-permute-start.3 = (f32[32,128]{1,0:T(8,128)S(1)}, f32[32,128]{1,0:T(8,128)S(1)}, u32[]{:S(2)}, u32[]{:S(2)}) collective-permute-start(f32[32,128]{1,0:T(8,128)S(1)} %get-tuple-element.17), channel_id=1, source_target_pairs={{0,2},{2,4},{4,6},{6,8},{8,10},{10,12},{12,14},{14,16},{16,18},{18... | collective-permute-start | bytes 49160 | tf_op jit(solution)/shard_map/ppermute | solution.py:490

commit v2 on v1

v2 whole, which is shorter than its diff:
```python
import functools

import jax
import jax.numpy as jnp
from jax import lax
from jax.experimental import pallas as pl
from jax.experimental.pallas import tpu as pltpu
from jax.sharding import PartitionSpec as P

advect_coef = 0.5
diffuse_coef = 0.25
twice_step = 0.5
gravity = 0.5
coriolis = 0.5
thermal = 0.2
haline = 0.15
asselin = 0.1

LANES = 128
SUBS = 8
FIELDS = 4
LEVELS = 4
ROWS = FIELDS * LEVELS
VMEM_LIMIT = 24 * 1024 * 1024

speed_coef = advect_coef * 0.5
ANY = pl.BlockSpec(memory_space=pl.ANY)
VMEM = pl.BlockSpec(memory_space=pltpu.VMEM)


def mask_of(field):
    return max(field - 1, 0)


def lane_ids(shape):
    return lax.broadcasted_iota(jnp.int32, shape, len(shape) - 1)


def row_ids(shape):
    return lax.broadcasted_iota(jnp.int32, shape, len(shape) - 2)


def edges_kernel(
    n_lat,
    earlier, present, scalar_flags, east_flags, north_flags,
    pay_a, pay_b, pay_west, pay_east, coef_north, coef_south, coef_west, coef_east,
    col_state, col_flag, row_state, row_flag, sems,
):
    height, width = present.shape[2], present.shape[3]
    lat = lax.axis_index("lat")
    flags = (scalar_flags, east_flags, north_flags)
    copies = []
    for side in range(2):
        cols = pl.ds(0 if side == 0 else width - LANES, LANES)
        for t, state in enumerate((present, earlier)):
            copies.append((state.at[:, :, :, cols], col_state.at[side, t]))
        for t, flag in enumerate(flags):
            copies.append((flag.at[:, :, cols], col_flag.at[side, t]))
    for side in range(2):
        rows = pl.ds(0 if side == 0 else height - SUBS, SUBS)
        for t, state in enumerate((present, earlier)):
            copies.append((state.at[:, :, rows, :], row_state.at[side, t]))
        for t, flag in enumerate(flags):
            copies.append((flag.at[:, rows, :], row_flag.at[side, t]))
    copies = [
        pltpu.make_async_copy(src, dst, sems.at[i]) for i, (src, dst) in enumerate(copies)
    ]
    for copy in copies:
        copy.start()
    n_tiles = width // LANES
    lane = lane_ids((SUBS, LANES))
    sub = row_ids((SUBS, LANES))

    for copy in copies[:10]:
        copy.wait()

    base, level = lane & (ROWS - 1), lane & (LEVELS - 1)
    zeros = jnp.zeros((SUBS, LANES), jnp.float32)
    tiles = range(height // SUBS)

    def columns(x, at):
        return [jnp.broadcast_to(x[r * SUBS : (r + 1) * SUBS, at : at + 1], (SUBS, LANES)) for r in tiles]

    def placed(where, xs, old):
        return [jnp.where(where, x, o) for x, o in zip(xs, old)]

    def col_pack(side, at):
        fm, both, extra, u, total = ([zeros] * len(tiles) for _ in range(5))
        for l in range(LEVELS):
            mask = [columns(col_flag[side, t, l].astype(jnp.float32), at) for t in range(3)]
            for f in range(FIELDS):
                fm = placed(base == f * LEVELS + l, mask[mask_of(f)], fm)
            now = []
            for f in range(FIELDS):
                now.append(columns(col_state[side, 0, f, l], at))
                both = placed(lane == f * LEVELS + l, now[f], both)
                both = placed(lane == ROWS + f * LEVELS + l, columns(col_state[side, 1, f, l], at), both)
            if side == 0:
                rho = [(haline * s - thermal * t) * m for s, t, m in zip(now[1], now[0], mask[0])]
                total = [a + b for a, b in zip(total, rho)]
                pres = [a - 0.5 * b for a, b in zip(total, rho)]
                extra = placed(lane == 2 * ROWS + 2 * LEVELS + l, pres, extra)
            else:
                extra = placed(level == l, mask[1], extra)
                u = placed(level == l, now[2], u)
        return zip(fm, both, extra, u)

    in_pres = (lane >= 2 * ROWS + 2 * LEVELS) & (lane < 2 * ROWS + 3 * LEVELS)
    going_west, going_east, coefs_west, coefs_east = [], [], [], []
    for fm, both, pres, _ in col_pack(0, 0):
        both = both * fm
        moved = pltpu.roll(both, ROWS, 1)
        going_west.append(both + pres)
        coefs_west.append(twice_step * jnp.where(lane < ROWS, fm, jnp.where(lane < 2 * ROWS, moved, -moved)))
    for fm, both, mu, u in col_pack(1, LANES - 1):
        s, dm = speed_coef * u * mu, diffuse_coef * mu
        own = both * fm * jnp.where(lane < ROWS, s, dm)
        g = own + pltpu.roll(own, LANES - ROWS, 1)
        going_east.append(jnp.where(lane < ROWS, g, jnp.where(lane < 2 * ROWS, s, dm)))
        face = jnp.where(lane < ROWS, -twice_step * s, twice_step * dm) * fm
        coefs_east.append(
            jnp.where(lane < 2 * ROWS, face, jnp.where(in_pres, -twice_step * gravity * mu, 0.0))
        )
    half = len(tiles) // 2
    folded = [
        [jnp.where(lane < LANES // 2, x[r], pltpu.roll(x[r + half], LANES // 2, 1)) for r in range(half)]
        for x in (going_west, going_east)
    ]
    for r in tiles:
        rows = pl.ds(r * SUBS, SUBS)
        coef_west[rows, :] = coefs_west[r]
        coef_east[rows, :] = coefs_east[r]
        if r < half:
            pay_west[rows, :] = folded[0][r]
            pay_east[rows, :] = folded[1][r]

    for copy in copies[10:]:
        copy.wait()

    def row_pack(side, at, j):
        line = pl.ds(at, 1)
        cols = pl.ds(j * LANES, LANES)

        def gather(rows):
            packed = jnp.broadcast_to(rows[0], (SUBS, LANES))
            for k in range(1, SUBS):
                packed = jnp.where(sub == k, jnp.broadcast_to(rows[k], (SUBS, LANES)), packed)
            return packed

        def flag_row(t, l):
            return row_flag[side, t, l, line, cols].astype(jnp.float32)

        fm = [
            gather([flag_row(mask_of(f), l) for f in (2 * h, 2 * h + 1) for l in range(LEVELS)])
            for h in range(2)
        ]
        cur, bef = (
            [
                fm[h]
                * gather([row_state[side, t, f, l, line, cols] for f in (2 * h, 2 * h + 1) for l in range(LEVELS)])
                for h in range(2)
            ]
            for t in range(2)
        )
        return fm, cur, bef

    back = LANES - 1 - lane
    pay_b[pl.ds(2 * ROWS * n_tiles, SUBS), :] = jnp.zeros((SUBS, LANES), jnp.float32)
    even = lat % 2 == 0
    is_top = lat == n_lat - 1
    for j in range(n_tiles):
        cols = pl.ds(j * LANES, LANES)
        fm, cur, bef = row_pack(1, SUBS - 1, j)
        low_v = pltpu.roll(cur[1], 4, 0)
        s = speed_coef * jnp.where(sub < 4, low_v, cur[1])
        m = diffuse_coef * jnp.where(sub < 4, pltpu.roll(fm[1], 4, 0), fm[1])
        g = [s * cur[h] + m * bef[h] for h in range(2)]
        for h in range(2):
            at = pl.ds(h * SUBS, SUBS)
            coef_north[at, cols] = -twice_step * fm[h] * s
            coef_north[pl.ds(ROWS + h * SUBS, SUBS), cols] = twice_step * fm[h] * m
        coef_north[pl.ds(2 * ROWS, SUBS), cols] = jnp.where(sub < 4, 0.0, -twice_step * gravity * fm[1])

        fm_s, cur_s, bef_s = row_pack(0, 0, j)
        for h in range(2):
            at = pl.ds(h * SUBS, SUBS)
            coef_south[at, cols] = twice_step * fm_s[h]
            coef_south[pl.ds(ROWS + h * SUBS, SUBS), cols] = twice_step * cur_s[h]
            coef_south[pl.ds(2 * ROWS + h * SUBS, SUBS), cols] = -twice_step * bef_s[h]

        north_going = g + [s, m]
        south_going = cur_s + bef_s
        for q in range(4):
            at = pl.ds(q * SUBS, SUBS)
            pay_a[at, cols] = jnp.where(even, north_going[q], south_going[q])

        @pl.when(jnp.logical_not(is_top))
        def _():
            for q in range(4):
                below = jnp.where(lat == 0, 0.0, south_going[q])
                pay_b[pl.ds((4 * j + q) * SUBS, SUBS), :] = jnp.where(even, below, north_going[q])

        @pl.when(is_top)
        def _():
            for q, x in enumerate(cur + bef):
                mirrored = pl.ds((4 * (n_tiles - 1 - j) + q) * SUBS, SUBS)
                turned = jnp.take_along_axis(x, back, axis=1)
                pay_b[mirrored, :] = turned if q % 2 == 0 else -turned


def inner_kernel(
    total_rows,
    raw_bef, raw_cur, scalar_flags, east_flags, north_flags,
    after_v, filtered_v,
    cur_v, bef_v, pres_v, flux_v,
):
    height, width = raw_cur.shape[2], raw_cur.shape[3]
    n_chunks, n_tiles = height // SUBS, width // LANES
    lat = lax.axis_index("lat")
    flags = (scalar_flags, east_flags, north_flags)

    zero = jnp.zeros((SUBS, LANES), jnp.float32)
    lane = lane_ids((SUBS, LANES))
    sub = row_ids((SUBS, LANES))
    first_lane, last_lane = lane == 0, lane == LANES - 1
    last_sub = sub == SUBS - 1
    tiles = [pl.ds(j * LANES, LANES) for j in range(n_tiles)]
    for l in range(LEVELS):
        for j in range(n_tiles):
            pres_v[l, j, pl.ds(height, SUBS), :] = zero
            for f in range(FIELDS):
                cur_v[f, l, j, pl.ds(height, SUBS), :] = zero
                bef_v[f, l, j, pl.ds(height, SUBS), :] = zero
                flux_v[f, l, j] = zero

    def store(puts):
        for ref, at, value in puts:
            ref[at] = value

    def each(op, *xs):
        return [op(*x) for x in zip(*xs)]

    def east_of(x):
        return [
            pltpu.roll(jnp.where(first_lane, b, a), LANES - 1, 1) for a, b in zip(x, x[1:] + [zero])
        ]

    def west_of(x):
        return [pltpu.roll(jnp.where(last_lane, b, a), 1, 1) for a, b in zip(x, [zero] + x[:-1])]

    def south_of(x, below):
        return [pltpu.roll(jnp.where(last_sub, b, a), 1, 0) for a, b in zip(x, below)]

    def face_flux(s, m, x, x_next, y, y_next):
        return each(lambda s, m, x, xn, y, yn: s * (x + xn) - m * (yn - y), s, m, x, x_next, y, y_next)

    def at(ref, r):
        return [ref[j, r, :] for j in range(n_tiles)]

    half = twice_step

    def unit(c, l, fields):
        rows = pl.ds(pl.multiple_of(c * SUBS, SUBS), SUBS)
        shifted = pl.ds(c * SUBS + 1, SUBS)

        def flag(t):
            return [flags[t][l, rows, cols].astype(jnp.float32) for cols in tiles]

        cur_e = {f: east_of(at(cur_v.at[f, l], rows)) for f in fields}
        bef_e = {f: east_of(at(bef_v.at[f, l], rows)) for f in fields}
        pres_e = east_of(at(pres_v.at[l], rows)) if 2 in fields else None
        yield []
        s_e, m_e = [half * speed_coef * x for x in at(cur_v.at[2, l], rows)], [half * diffuse_coef * x for x in flag(1)]
        s_n, m_n = [half * speed_coef * x for x in at(cur_v.at[3, l], rows)], [half * diffuse_coef * x for x in flag(2)]
        puts, own, west, south = [], {}, {}, {}
        for f in fields:
            cur, bef = at(cur_v.at[f, l], rows), at(bef_v.at[f, l], rows)
            flux_e = face_flux(s_e, m_e, cur, cur_e[f], bef, bef_e[f])
            flux_n = face_flux(s_n, m_n, cur, at(cur_v.at[f, l], shifted), bef, at(bef_v.at[f, l], shifted))
            west[f] = west_of(flux_e)
            south[f] = south_of(flux_n, at(flux_v.at[f, l], slice(None)))
            own[f] = each(lambda e, n: e + n, flux_e, flux_n)
            puts += [(flux_v, (f, l, j), x) for j, x in enumerate(flux_n)]
        yield puts
        puts = []
        for f in fields:
            cur, bef = at(cur_v.at[f, l], rows), at(bef_v.at[f, l], rows)
            mask = flag(mask_of(f))
            tend = each(lambda w, s, o: (w + s) - o, west[f], south[f], own[f])
            if f >= 2:
                index = (lat * height + c * SUBS + sub).astype(jnp.float32)
                cor = half * coriolis * (2.0 * (index + 0.5) / total_rows - 1.0)
                pres = at(pres_v.at[l], rows)
                ahead = pres_e if f == 2 else at(pres_v.at[l], shifted)
                slope = each(lambda m, a, p: (half * gravity) * m * (a - p), mask, ahead, pres)
                if f == 2:
                    tend = each(lambda t, v, g: t + (cor * v - g), tend, at(cur_v.at[3, l], rows), slope)
                else:
                    tend = each(lambda t, u, g: t - (cor * u + g), tend, at(cur_v.at[2, l], rows), slope)
            new = each(lambda b, t, m: (b + t) * m, bef, tend, mask)
            mid = each(lambda c, b, n: (1.0 - 2.0 * asselin) * c + asselin * (b + n), cur, bef, new)
            for cols, a, x in zip(tiles, new, mid):
                puts.append((after_v, (f, l, rows, cols), a))
                puts.append((filtered_v, (f, l, rows, cols), x))
        yield puts

    def masking(c):
        rows = pl.ds(pl.multiple_of(c * SUBS, SUBS), SUBS)
        totals = [zero] * n_tiles
        for l in range(LEVELS):
            for part in (range(0, n_tiles // 2), range(n_tiles // 2, n_tiles)):
                puts = []
                for j in part:
                    cols = tiles[j]
                    masks = [flags[t][l, rows, cols].astype(jnp.float32) for t in range(3)]
                    cur = [raw_cur[f, l, rows, cols] * masks[mask_of(f)] for f in range(FIELDS)]
                    rho = haline * cur[1] - thermal * cur[0]
                    totals[j] = totals[j] + rho
                    puts.append((pres_v, (l, j, rows), totals[j] - 0.5 * rho))
                    for f in range(FIELDS):
                        puts.append((cur_v, (f, l, j, rows), cur[f]))
                        puts.append((bef_v, (f, l, j, rows), raw_bef[f, l, rows, cols] * masks[mask_of(f)]))
                yield puts

    for c in range(2):
        for puts in masking(c):
            store(puts)

    def two_chunks(i, carry):
        units = [unit(2 * i + k, l, fields) for k in range(2) for l in range(LEVELS) for fields in ((0, 1), (2, 3))]
        later = [masking(jnp.minimum(2 * i + 2 + k, n_chunks - 1)) for k in range(2)]
        per_chunk = len(units) // 2
        for t in range(len(units) + 2):
            puts = []
            for u in (t, t - 1, t - 2):
                if 0 <= u < len(units):
                    puts += next(units[u])
            if t < len(units):
                puts += next(later[t // per_chunk])
            store(puts)
        return carry

    lax.fori_loop(0, n_chunks // 2, two_chunks, 0)


def rim_kernel(
    got_a, got_b, got_east, got_west, coef_north, coef_south, coef_west, coef_east,
    after_v, filtered_v,
    after, filtered, after_w, filtered_w,
    add_rows, add_cols, sems,
):
    height, width = after.shape[2], after.shape[3]
    n_chunks, n_tiles = height // SUBS, width // LANES
    lane = lane_ids((SUBS, LANES))
    sub = row_ids((SUBS, LANES))
    even = lax.axis_index("lat") % 2 == 0

    def out(i, rows, cols):
        copies = [
            pltpu.make_async_copy(s.at[:, :, rows, cols], d.at[:, :, rows, cols], sems.at[i, q])
            for q, (s, d) in enumerate(((after_w, after), (filtered_w, filtered)))
        ]
        for copy in copies:
            copy.start()
        return copies

    middle = pl.ds(SUBS, height - 2 * SUBS)
    pending = out(2, middle, pl.ds(LANES, width - 2 * LANES))

    for j in range(n_tiles):
        cols = pl.ds(j * LANES, LANES)
        got = [(got_a[pl.ds(q * SUBS, SUBS), cols], got_b[pl.ds((4 * j + q) * SUBS, SUBS), :]) for q in range(4)]
        north = [jnp.where(even, a, b) for a, b in got]
        south = [jnp.where(even, b, a) for a, b in got]

        def coef(ref, q):
            return ref[pl.ds(q * SUBS, SUBS), cols]

        rho = jnp.where(sub < LEVELS, haline * pltpu.roll(north[0], LEVELS, 0) - thermal * north[0], 0.0)
        total = rho + pltpu.roll(rho, 1, 0)
        total = total + pltpu.roll(total, 2, 0)
        pres = pltpu.roll(total - 0.5 * rho, LEVELS, 0)
        for h in range(2):
            at = pl.ds(h * SUBS, SUBS)
            up = coef(coef_north, h) * north[h] + coef(coef_north, 2 + h) * north[2 + h]
            if h == 1:
                up = up + coef(coef_north, 4) * pres
            add_rows[1, at, cols] = up
            add_rows[0, at, cols] = (
                coef(coef_south, h) * south[h]
                + coef(coef_south, 2 + h) * south[2]
                + coef(coef_south, 4 + h) * south[3]
            )

    for side, (got, coef) in enumerate(((got_west[...], coef_west), (got_east[...], coef_east))):
        for part in range(2):
            rows = pl.ds(part * (height // 2), height // 2)
            x = got if part == 0 else pltpu.roll(got, LANES // 2, 1)
            x = x * coef[rows, :]
            add_cols[side, rows, :] = (
                x + pltpu.roll(x, LANES - ROWS, 1) + pltpu.roll(x, LANES - 2 * ROWS, 1)
            )

    def edge_cols(rows):
        return add_cols[0, rows, :], add_cols[1, rows, :]

    def put(value, k, at):
        return jnp.where(lane == at, jnp.broadcast_to(value[:, k : k + 1], (SUBS, LANES)), 0.0)

    def apply(extras):
        sums = [(at, after_v[at] + x, filtered_v[at] + asselin * x) for at, x in extras]
        for at, new, mid in sums:
            after_w[at] = new
            filtered_w[at] = mid

    def row_chunk(c, side, line):
        rows = pl.ds(c * SUBS, SUBS)
        west, east = edge_cols(rows)
        for f in range(FIELDS):
            extras = []
            for l in range(LEVELS):
                k = f * LEVELS + l
                for j in range(n_tiles):
                    cols = pl.ds(j * LANES, LANES)
                    extra = jnp.where(sub == line, jnp.broadcast_to(add_rows[side, pl.ds(k, 1), cols], (SUBS, LANES)), 0.0)
                    if j == 0:
                        extra = extra + put(west, k, 0)
                    if j == n_tiles - 1:
                        extra = extra + put(east, k, LANES - 1)
                    extras.append(((f, l, rows, cols), extra))
            apply(extras)

    def side_chunk(c):
        first, last = pl.ds(0, LANES), pl.ds(width - LANES, LANES)
        tiles = [pl.ds(pl.multiple_of(r * SUBS, SUBS), SUBS) for r in (c, c + 1)]
        edges = [edge_cols(rows) for rows in tiles]
        for f in range(FIELDS):
            extras = []
            for l in range(LEVELS):
                k = f * LEVELS + l
                for rows, (west, east) in zip(tiles, edges):
                    extras.append(((f, l, rows, first), put(west, k, 0)))
                    extras.append(((f, l, rows, last), put(east, k, LANES - 1)))
            apply(extras)

    row_chunk(0, 0, 0)
    pending += out(0, pl.ds(0, SUBS), pl.ds(0, width))
    row_chunk(n_chunks - 1, 1, SUBS - 1)
    pending += out(1, pl.ds(height - SUBS, SUBS), pl.ds(0, width))
    for c in range(1, n_chunks - 1, 2):
        side_chunk(c)
        rows = pl.ds(c * SUBS, 2 * SUBS)
        pending += out(2 + c, rows, pl.ds(0, LANES))
        pending += out(3 + c, rows, pl.ds(width - LANES, LANES))
    for copy in pending:
        copy.wait()


def shards(n_lat, earlier_state, present_state, scalar_wet_flags, eastside_wet_flags, northside_wet_flags):
    args = (earlier_state, present_state, scalar_wet_flags, eastside_wet_flags, northside_wet_flags)
    height, width = present_state.shape[2:]
    n_lon = lax.axis_size("lon")
    f32 = jnp.float32
    params = pltpu.CompilerParams(vmem_limit_bytes=VMEM_LIMIT)
    state = (FIELDS, LEVELS, height, width)
    apart = (LEVELS, width // LANES, height + SUBS, LANES)

    def vmem(*shape):
        return pltpu.VMEM(shape, f32)

    edges = pl.pallas_call(
        functools.partial(edges_kernel, n_lat),
        out_shape=[
            vmem(2 * ROWS, width), vmem(2 * ROWS * (width // LANES) + SUBS, LANES),
            vmem(height // 2, LANES), vmem(height // 2, LANES),
            vmem(2 * ROWS + SUBS, width), vmem(3 * ROWS, width), vmem(height, LANES), vmem(height, LANES),
        ],
        in_specs=[ANY] * 5,
        out_specs=[VMEM] * 8,
        scratch_shapes=[
            pltpu.VMEM((2, 2, FIELDS, LEVELS, height, LANES), f32),
            pltpu.VMEM((2, 3, LEVELS, height, LANES), jnp.int32),
            pltpu.VMEM((2, 2, FIELDS, LEVELS, SUBS, width), f32),
            pltpu.VMEM((2, 3, LEVELS, SUBS, width), jnp.int32),
            pltpu.SemaphoreType.DMA((20,)),
        ],
        compiler_params=params,
        cost_estimate=pl.CostEstimate(flops=500_000, bytes_accessed=3_600_000, transcendentals=0),
        name="edges",
    )(*[pltpu.with_memory_space_constraint(x, pltpu.HBM) for x in args])
    pay_a, pay_b, pay_west, pay_east, *coefs = edges

    def device(lon, lat):
        return lon * n_lat + lat

    lons, lats, top = range(n_lon), range(n_lat), n_lat - 1
    pairs_a = [(device(lon, lat), device(lon, lat ^ 1)) for lon in lons for lat in lats]
    pairs_b = [
        (
            device(lon, lat),
            device(n_lon - 1 - lon, lat) if lat in (0, top) else device(lon, lat + 1 if lat % 2 else lat - 1),
        )
        for lon in lons
        for lat in lats
    ]
    got_b = lax.ppermute(pay_b, ("lon", "lat"), pairs_b)
    got_a = lax.ppermute(pay_a, ("lon", "lat"), pairs_a)
    got_east = lax.ppermute(pay_west, "lon", [(i, (i - 1) % n_lon) for i in lons])
    got_west = lax.ppermute(pay_east, "lon", [(i, (i + 1) % n_lon) for i in lons])

    after_v, filtered_v = pl.pallas_call(
        functools.partial(inner_kernel, height * n_lat),
        out_shape=[vmem(*state), vmem(*state)],
        in_specs=[VMEM] * 5,
        out_specs=[VMEM, VMEM],
        scratch_shapes=[
            pltpu.VMEM((FIELDS, *apart), f32),
            pltpu.VMEM((FIELDS, *apart), f32),
            pltpu.VMEM(apart, f32),
            pltpu.VMEM((FIELDS, LEVELS, width // LANES, SUBS, LANES), f32),
        ],
        compiler_params=params,
        cost_estimate=pl.CostEstimate(flops=20_000_000, bytes_accessed=9_000_000, transcendentals=0),
        name="inner",
    )(*[pltpu.with_memory_space_constraint(x, pltpu.VMEM) for x in args])

    def in_vmem(x):
        return pltpu.with_memory_space_constraint(x, pltpu.VMEM)

    fixed = [in_vmem(x) for x in (got_a, got_b, got_east, got_west, *coefs, after_v, filtered_v)]
    after, filtered, _, _ = pl.pallas_call(
        rim_kernel,
        out_shape=[pltpu.HBM(state, f32), pltpu.HBM(state, f32), vmem(*state), vmem(*state)],
        in_specs=[VMEM] * 10,
        out_specs=[ANY, ANY, VMEM, VMEM],
        scratch_shapes=[
            pltpu.VMEM((2, ROWS, width), f32),
            pltpu.VMEM((2, height, LANES), f32),
            pltpu.SemaphoreType.DMA((3 + height // SUBS, 2)),
        ],
        input_output_aliases={8: 2, 9: 3},
        compiler_params=params,
        cost_estimate=pl.CostEstimate(flops=500_000, bytes_accessed=3_000_000, transcendentals=0),
        name="rim",
    )(*fixed)
    return after, filtered


def solution(mesh):
    placed = (
        P(None, None, "lat", "lon"),
        P(None, None, "lat", "lon"),
        P(None, "lat", "lon"),
        P(None, "lat", "lon"),
        P(None, "lat", "lon"),
    )
    return jax.shard_map(
        functools.partial(shards, mesh.shape["lat"]),
        mesh=mesh,
        in_specs=placed,
        out_specs=(P(None, None, "lat", "lon"), P(None, None, "lat", "lon")),
        check_vma=False,
    )
```

time: 23.5 us -> 19.7 us (0.84)
  the two profiles are of different devices: /device:TPU:1 before, /device:TPU:0 now
where the time goes in v2:
time: 19.7 us; the launch traced here: 19.5 us
  Pallas kernels  9.59 us (49%)
  starting transfers between devices  7.78 us (39%)
  waiting for transfers between devices  1.4 us (7%)
  between operations  0.71 us (4%)
    ppermute x1, starting transfers between devices, shards(): got_b = lax.ppermute(pay_b, ('lon', 'lat'), pairs_b)  5.48 us
    pallas_call x1, Pallas kernels, shards(): pl.pallas_call(functools.partial(inner_kernel, height * n_lat), out_shape...  4.11 us
    pallas_call x1, Pallas kernels, shards(): pl.pallas_call(functools.partial(edges_kernel, n_lat), out_shape=[vmem(2...  3.3 us
    pallas_call x1, Pallas kernels, shards(): pl.pallas_call(rim_kernel, out_shape=[pltpu.HBM(state, f32), pltpu.HBM(st...  2.18 us
    ppermute x1, starting transfers between devices, shards(): got_a = lax.ppermute(pay_a, ('lon', 'lat'), pairs_a)  1.79 us
    ppermute x1, waiting for transfers between devices, shards(): lax.ppermute(pay_east, 'lon', [(i, (i + 1) % n_lon) for i in lons])  1.39 us
  transfers between devices with their start and end apart: 4, of which 1 were waited for; matrix products, arithmetic and copies ran while one was open for 0% of the time, Pallas kernels for 21%

profile of v2, /device:TPU:0, one launch (start us, length us, event | category | flops | bytes accessed | tf_op | source)
XLA Modules:
  0.0 19.5 jit_solution(13035159232014193974)
XLA Ops:
  0.6 0.0 copy-start.4
  0.6 0.0 copy-start.3
  0.7 0.0 copy-start.2
  0.7 0.0 copy-start.1
  0.7 0.0 copy-start
  0.7 3.3 %edges.1 = (f32[32,512]{1,0:T(8,128)S(1)}, f32[136,128]{1,0:T(8,128)S(1)}, f32[32,128]{1,0:T(8,128)S(1)}, f32[32,128]{1,0:T(8,128)S(1)}, f32[40,512]{1,0:T(8,128...) custom-call(f32[4,4,64,512]{3,2,1,0:T(8,128)} %raw_bef.1, f32[4,4,64,512]{3,2,1,0:T(8,128)} %raw_cur.1, ...), custom_call_target="tpu_custom_call" | custom-call | flops 500000 | bytes 3600000 | tf_op jit(solution)/shard_map/edges/pallas_call | solution.py:471
  4.0 5.5 %collective-permute-start.1 = (f32[136,128]{1,0:T(8,128)S(1)}, f32[136,128]{1,0:T(8,128)S(1)}, u32[]{:S(2)}, u32[]{:S(2)}) collective-permute-start(f32[136,128]{1,0:T(8,128)S(1)} %get-tuple-element.15), channel_id=1, source_target_pairs={{0,30},{1,31},{2,28},{3,29},{4,26},{5,27},{6,24},{7,25},{8,22},{9,... | collective-permute-start | bytes 208904 | tf_op jit(solution)/shard_map/ppermute | solution.py:506
  9.5 1.8 %collective-permute-start = (f32[32,512]{1,0:T(8,128)S(1)}, f32[32,512]{1,0:T(8,128)S(1)}, u32[]{:S(2)}, u32[]{:S(2)}) collective-permute-start(f32[32,512]{1,0:T(8,128)S(1)} %get-tuple-element.14), channel_id=1, source_target_pairs={{0,1},{1,0},{2,3},{3,2},{4,5},{5,4},{6,7},{7,6},{8,9},{9,8},{10,11... | collective-permute-start | bytes 196616 | tf_op jit(solution)/shard_map/ppermute | solution.py:507
  11.3 0.2 collective-permute-start.2
  11.5 0.3 %collective-permute-start.3 = (f32[32,128]{1,0:T(8,128)S(1)}, f32[32,128]{1,0:T(8,128)S(1)}, u32[]{:S(2)}, u32[]{:S(2)}) collective-permute-start(f32[32,128]{1,0:T(8,128)S(1)} %get-tuple-element.17), channel_id=1, source_target_pairs={{0,2},{2,4},{4,6},{6,8},{8,10},{10,12},{12,14},{14,16},{16,18},{18... | collective-permute-start | bytes 49160 | tf_op jit(solution)/shard_map/ppermute | solution.py:509
  11.8 0.0 copy-done.4
  11.8 0.0 copy-done.3
  11.8 0.0 copy-done.2
  11.8 0.0 copy-done.1
  11.8 0.0 copy-done
  11.8 4.1 %inner.1 = (f32[4,4,64,512]{3,2,1,0:T(8,128)S(1)}, f32[4,4,64,512]{3,2,1,0:T(8,128)S(1)}) custom-call(f32[4,4,64,512]{3,2,1,0:T(8,128)S(1)} %copy-done, f32[4,4,64,512]{3,2,1,0:T(8,128)S(1)} %copy-done.1, s32[4,64,512]{2,1,0:T(8,128)S(1)} %copy-done.2, s32[4,64,512]{2,1,0:T(8,128)S(1)} %copy-done.3, s32[4,64,512]{2,1,0:T(8,128)S(1)} %copy-done.4), custom_call_target="tpu_custom_call" | custom-call | flops 20000000 | bytes 9000000 | tf_op jit(solution)/shard_map/inner/pallas_call | solution.py:511
  15.9 0.0 collective-permute-done.2.got_east
  15.9 1.4 %collective-permute-done.3.got_west = f32[32,128]{1,0:T(8,128)S(1)} collective-permute-done((f32[32,128]{1,0:T(8,128)S(1)}, f32[32,128]{1,0:T(8,128)S(1)}, u32[]{:S(2)}, u32[]{:S(2)}) %collective-permute-start.3) | collective-permute-done | bytes 16416 | tf_op jit(solution)/shard_map/ppermute | solution.py:509
  17.3 0.0 collective-permute-done.got_a
  17.3 0.0 collective-permute-done.1.got_b
  17.3 2.2 %rim.1 = (f32[4,4,64,512]{3,2,1,0:T(8,128)}, f32[4,4,64,512]{3,2,1,0:T(8,128)}, f32[4,4,64,512]{3,2,1,0:T(8,128)S(1)}, f32[4,4,64,512]{3,2,1,0:T(8,128)S(1)}) custom-call(f32[32,512]{1,0:T(8,128)S(1)} %collective-permute-done.got_a, f32[136,128]{1,0:T(8,128)S(1)} %collective-permute-done.1.got_b, ...), custom_call_target="tpu_custom_call", output_to_operand_aliasing={{2}: (8, {}), {3}: (9, {})} | custom-call | flops 500000 | bytes 3000000 | tf_op jit(solution)/shard_map/rim/pallas_call | solution.py:531
Async XLA Ops:
  0.6 11.1 %copy-start.4 = (s32[4,64,512]{2,1,0:T(8,128)S(1)}, s32[4,64,512]{2,1,0:T(8,128)}, u32[]{:S(2)}) copy-start(s32[4,64,512]{2,1,0:T(8,128)} %north_flags.3) | copy-start | bytes 1572868
  0.6 11.1 %copy-start.3 = (s32[4,64,512]{2,1,0:T(8,128)S(1)}, s32[4,64,512]{2,1,0:T(8,128)}, u32[]{:S(2)}) copy-start(s32[4,64,512]{2,1,0:T(8,128)} %east_flags.3) | copy-start | bytes 1572868
  0.7 11.1 %copy-start.2 = (s32[4,64,512]{2,1,0:T(8,128)S(1)}, s32[4,64,512]{2,1,0:T(8,128)}, u32[]{:S(2)}) copy-start(s32[4,64,512]{2,1,0:T(8,128)} %scalar_flags.3) | copy-start | bytes 1572868
  0.7 11.1 %copy-start.1 = (f32[4,4,64,512]{3,2,1,0:T(8,128)S(1)}, f32[4,4,64,512]{3,2,1,0:T(8,128)}, u32[]{:S(2)}) copy-start(f32[4,4,64,512]{3,2,1,0:T(8,128)} %raw_cur.1) | copy-start | bytes 6291460
  0.7 11.1 %copy-start = (f32[4,4,64,512]{3,2,1,0:T(8,128)S(1)}, f32[4,4,64,512]{3,2,1,0:T(8,128)}, u32[]{:S(2)}) copy-start(f32[4,4,64,512]{3,2,1,0:T(8,128)} %raw_bef.1) | copy-start | bytes 6291460
  4.0 13.3 %collective-permute-start.1 = (f32[136,128]{1,0:T(8,128)S(1)}, f32[136,128]{1,0:T(8,128)S(1)}, u32[]{:S(2)}, u32[]{:S(2)}) collective-permute-start(f32[136,128]{1,0:T(8,128)S(1)} %get-tuple-element.15), channel_id=1, source_target_pairs={{0,30},{1,31},{2,28},{3,29},{4,26},{5,27},{6,24},{7,25},{8,22},{9,... | collective-permute-start | bytes 208904 | tf_op jit(solution)/shard_map/ppermute | solution.py:506
  9.5 7.8 %collective-permute-start = (f32[32,512]{1,0:T(8,128)S(1)}, f32[32,512]{1,0:T(8,128)S(1)}, u32[]{:S(2)}, u32[]{:S(2)}) collective-permute-start(f32[32,512]{1,0:T(8,128)S(1)} %get-tuple-element.14), channel_id=1, source_target_pairs={{0,1},{1,0},{2,3},{3,2},{4,5},{5,4},{6,7},{7,6},{8,9},{9,8},{10,11... | collective-permute-start | bytes 196616 | tf_op jit(solution)/shard_map/ppermute | solution.py:507
  11.3 4.7 %collective-permute-start.2 = (f32[32,128]{1,0:T(8,128)S(1)}, f32[32,128]{1,0:T(8,128)S(1)}, u32[]{:S(2)}, u32[]{:S(2)}) collective-permute-start(f32[32,128]{1,0:T(8,128)S(1)} %get-tuple-element.16), channel_id=1, source_target_pairs={{0,30},{2,0},{4,2},{6,4},{8,6},{10,8},{12,10},{14,12},{16,14},{18,... | collective-permute-start | bytes 49160 | tf_op jit(solution)/shard_map/ppermute | solution.py:508
  11.5 5.9 %collective-permute-start.3 = (f32[32,128]{1,0:T(8,128)S(1)}, f32[32,128]{1,0:T(8,128)S(1)}, u32[]{:S(2)}, u32[]{:S(2)}) collective-permute-start(f32[32,128]{1,0:T(8,128)S(1)} %get-tuple-element.17), channel_id=1, source_target_pairs={{0,2},{2,4},{4,6},{6,8},{8,10},{10,12},{12,14},{14,16},{16,18},{18... | collective-permute-start | bytes 49160 | tf_op jit(solution)/shard_map/ppermute | solution.py:509

commit v3 on v2

--- a/solution.py
+++ b/solution.py
@@ -165,47 +165,39 @@
         return fm, cur, bef
 
     back = LANES - 1 - lane
-    pay_b[pl.ds(2 * ROWS * n_tiles, SUBS), :] = jnp.zeros((SUBS, LANES), jnp.float32)
     even = lat % 2 == 0
     is_top = lat == n_lat - 1
+    puts = [(pay_b, pl.ds(2 * ROWS * n_tiles, SUBS), slice(None), zeros)]
+    into_b, folded = [], []
     for j in range(n_tiles):
         cols = pl.ds(j * LANES, LANES)
         fm, cur, bef = row_pack(1, SUBS - 1, j)
-        low_v = pltpu.roll(cur[1], 4, 0)
-        s = speed_coef * jnp.where(sub < 4, low_v, cur[1])
+        s = speed_coef * jnp.where(sub < 4, pltpu.roll(cur[1], 4, 0), cur[1])
         m = diffuse_coef * jnp.where(sub < 4, pltpu.roll(fm[1], 4, 0), fm[1])
         g = [s * cur[h] + m * bef[h] for h in range(2)]
         for h in range(2):
-            at = pl.ds(h * SUBS, SUBS)
-            coef_north[at, cols] = -twice_step * fm[h] * s
-            coef_north[pl.ds(ROWS + h * SUBS, SUBS), cols] = twice_step * fm[h] * m
-        coef_north[pl.ds(2 * ROWS, SUBS), cols] = jnp.where(sub < 4, 0.0, -twice_step * gravity * fm[1])
+            puts.append((coef_north, pl.ds(h * SUBS, SUBS), cols, -twice_step * fm[h] * s))
+            puts.append((coef_north, pl.ds(ROWS + h * SUBS, SUBS), cols, twice_step * fm[h] * m))
+        puts.append((coef_north, pl.ds(2 * ROWS, SUBS), cols, jnp.where(sub < 4, 0.0, -twice_step * gravity * fm[1])))
 
         fm_s, cur_s, bef_s = row_pack(0, 0, j)
         for h in range(2):
-            at = pl.ds(h * SUBS, SUBS)
-            coef_south[at, cols] = twice_step * fm_s[h]
-            coef_south[pl.ds(ROWS + h * SUBS, SUBS), cols] = twice_step * cur_s[h]
-            coef_south[pl.ds(2 * ROWS + h * SUBS, SUBS), cols] = -twice_step * bef_s[h]
-
-        north_going = g + [s, m]
-        south_going = cur_s + bef_s
+            puts.append((coef_south, pl.ds(h * SUBS, SUBS), cols, twice_step * fm_s[h]))
+            puts.append((coef_south, pl.ds(ROWS + h * SUBS, SUBS), cols, twice_step * cur_s[h]))
+            puts.append((coef_south, pl.ds(2 * ROWS + h * SUBS, SUBS), cols, -twice_step * bef_s[h]))
+
+        north_going, south_going = g + [s, m], cur_s + bef_s
         for q in range(4):
-            at = pl.ds(q * SUBS, SUBS)
-            pay_a[at, cols] = jnp.where(even, north_going[q], south_going[q])
-
-        @pl.when(jnp.logical_not(is_top))
-        def _():
-            for q in range(4):
-                below = jnp.where(lat == 0, 0.0, south_going[q])
-                pay_b[pl.ds((4 * j + q) * SUBS, SUBS), :] = jnp.where(even, below, north_going[q])
-
-        @pl.when(is_top)
-        def _():
-            for q, x in enumerate(cur + bef):
-                mirrored = pl.ds((4 * (n_tiles - 1 - j) + q) * SUBS, SUBS)
-                turned = jnp.take_along_axis(x, back, axis=1)
-                pay_b[mirrored, :] = turned if q % 2 == 0 else -turned
+            puts.append((pay_a, pl.ds(q * SUBS, SUBS), cols, jnp.where(even, north_going[q], south_going[q])))
+        into_b.append([jnp.where(even, jnp.where(lat == 0, 0.0, y), x) for x, y in zip(north_going, south_going)])
+        turned = [jnp.take_along_axis(x, back, axis=1) for x in cur + bef]
+        folded.append([x if q % 2 == 0 else -x for q, x in enumerate(turned)])
+    for j in range(n_tiles):
+        for q in range(4):
+            value = jnp.where(is_top, folded[n_tiles - 1 - j][q], into_b[j][q])
+            puts.append((pay_b, pl.ds((4 * j + q) * SUBS, SUBS), slice(None), value))
+    for ref, rows, cols, value in puts:
+        ref[rows, cols] = value
 
 
 def inner_kernel(
@@ -327,7 +319,7 @@
             store(puts)
 
     def two_chunks(i, carry):
-        units = [unit(2 * i + k, l, fields) for k in range(2) for l in range(LEVELS) for fields in ((0, 1), (2, 3))]
+        units = [unit(2 * i + k, l, range(FIELDS)) for k in range(2) for l in range(LEVELS)]
         later = [masking(jnp.minimum(2 * i + 2 + k, n_chunks - 1)) for k in range(2)]
         per_chunk = len(units) // 2
         for t in range(len(units) + 2):
@@ -336,7 +328,7 @@
                 if 0 <= u < len(units):
                     puts += next(units[u])
             if t < len(units):
-                puts += next(later[t // per_chunk])
+                puts += next(later[t // per_chunk]) + next(later[t // per_chunk])
             store(puts)
         return carry
 

time: 19.7 us -> 19.4 us (0.985)
  starting transfers between devices: 7.78 us -> 7.51 us
    ppermute x1, starting transfers between devices: 1.79 us -> 1.52 us  [shards(): got_a = lax.ppermute(pay_a, ('lon', 'lat'), pairs_a)]
where the time goes in v3:
time: 19.4 us; the launch traced here: 19.2 us
  Pallas kernels  9.46 us (49%)
  starting transfers between devices  7.51 us (39%)
  waiting for transfers between devices  1.51 us (8%)
  between operations  0.71 us (4%)
    ppermute x1, starting transfers between devices, shards(): got_b = lax.ppermute(pay_b, ('lon', 'lat'), pairs_b)  5.48 us
    pallas_call x1, Pallas kernels, shards(): pl.pallas_call(functools.partial(inner_kernel, height * n_lat), out_shape...  4 us
    pallas_call x1, Pallas kernels, shards(): pl.pallas_call(functools.partial(edges_kernel, n_lat), out_shape=[vmem(2...  3.28 us
    pallas_call x1, Pallas kernels, shards(): pl.pallas_call(rim_kernel, out_shape=[pltpu.HBM(state, f32), pltpu.HBM(st...  2.18 us
    ppermute x1, starting transfers between devices, shards(): got_a = lax.ppermute(pay_a, ('lon', 'lat'), pairs_a)  1.52 us
    ppermute x1, waiting for transfers between devices, shards(): lax.ppermute(pay_east, 'lon', [(i, (i + 1) % n_lon) for i in lons])  1.5 us
  transfers between devices with their start and end apart: 4, of which 1 were waited for; matrix products, arithmetic and copies ran while one was open for 0% of the time, Pallas kernels for 21%

profile of v3, /device:TPU:0, one launch (start us, length us, event | category | flops | bytes accessed | tf_op | source)
XLA Modules:
  0.0 19.2 jit_solution(15540445344797348204)
XLA Ops:
  0.6 0.0 copy-start.4
  0.6 0.0 copy-start.3
  0.7 0.0 copy-start.2
  0.7 0.0 copy-start.1
  0.7 0.0 copy-start
  0.7 3.3 %edges.1 = (f32[32,512]{1,0:T(8,128)S(1)}, f32[136,128]{1,0:T(8,128)S(1)}, f32[32,128]{1,0:T(8,128)S(1)}, f32[32,128]{1,0:T(8,128)S(1)}, f32[40,512]{1,0:T(8,128...) custom-call(f32[4,4,64,512]{3,2,1,0:T(8,128)} %raw_bef.1, f32[4,4,64,512]{3,2,1,0:T(8,128)} %raw_cur.1, ...), custom_call_target="tpu_custom_call" | custom-call | flops 500000 | bytes 3600000 | tf_op jit(solution)/shard_map/edges/pallas_call | solution.py:463
  4.0 5.5 %collective-permute-start.1 = (f32[136,128]{1,0:T(8,128)S(1)}, f32[136,128]{1,0:T(8,128)S(1)}, u32[]{:S(2)}, u32[]{:S(2)}) collective-permute-start(f32[136,128]{1,0:T(8,128)S(1)} %get-tuple-element.15), channel_id=1, source_target_pairs={{0,30},{1,31},{2,28},{3,29},{4,26},{5,27},{6,24},{7,25},{8,22},{9,... | collective-permute-start | bytes 208904 | tf_op jit(solution)/shard_map/ppermute | solution.py:498
  9.4 1.5 %collective-permute-start = (f32[32,512]{1,0:T(8,128)S(1)}, f32[32,512]{1,0:T(8,128)S(1)}, u32[]{:S(2)}, u32[]{:S(2)}) collective-permute-start(f32[32,512]{1,0:T(8,128)S(1)} %get-tuple-element.14), channel_id=1, source_target_pairs={{0,1},{1,0},{2,3},{3,2},{4,5},{5,4},{6,7},{7,6},{8,9},{9,8},{10,11... | collective-permute-start | bytes 196616 | tf_op jit(solution)/shard_map/ppermute | solution.py:499
  11.0 0.2 %collective-permute-start.2 = (f32[32,128]{1,0:T(8,128)S(1)}, f32[32,128]{1,0:T(8,128)S(1)}, u32[]{:S(2)}, u32[]{:S(2)}) collective-permute-start(f32[32,128]{1,0:T(8,128)S(1)} %get-tuple-element.16), channel_id=1, source_target_pairs={{0,30},{2,0},{4,2},{6,4},{8,6},{10,8},{12,10},{14,12},{16,14},{18,... | collective-permute-start | bytes 49160 | tf_op jit(solution)/shard_map/ppermute | solution.py:500
  11.2 0.3 %collective-permute-start.3 = (f32[32,128]{1,0:T(8,128)S(1)}, f32[32,128]{1,0:T(8,128)S(1)}, u32[]{:S(2)}, u32[]{:S(2)}) collective-permute-start(f32[32,128]{1,0:T(8,128)S(1)} %get-tuple-element.17), channel_id=1, source_target_pairs={{0,2},{2,4},{4,6},{6,8},{8,10},{10,12},{12,14},{14,16},{16,18},{18... | collective-permute-start | bytes 49160 | tf_op jit(solution)/shard_map/ppermute | solution.py:501
  11.5 0.0 copy-done.4
  11.5 0.0 copy-done.3
  11.5 0.0 copy-done.2
  11.5 0.0 copy-done.1
  11.5 0.0 copy-done
  11.5 4.0 %inner.1 = (f32[4,4,64,512]{3,2,1,0:T(8,128)S(1)}, f32[4,4,64,512]{3,2,1,0:T(8,128)S(1)}) custom-call(f32[4,4,64,512]{3,2,1,0:T(8,128)S(1)} %copy-done, f32[4,4,64,512]{3,2,1,0:T(8,128)S(1)} %copy-done.1, s32[4,64,512]{2,1,0:T(8,128)S(1)} %copy-done.2, s32[4,64,512]{2,1,0:T(8,128)S(1)} %copy-done.3, s32[4,64,512]{2,1,0:T(8,128)S(1)} %copy-done.4), custom_call_target="tpu_custom_call" | custom-call | flops 20000000 | bytes 9000000 | tf_op jit(solution)/shard_map/inner/pallas_call | solution.py:503
  15.5 0.0 collective-permute-done.2.got_east
  15.5 1.5 %collective-permute-done.3.got_west = f32[32,128]{1,0:T(8,128)S(1)} collective-permute-done((f32[32,128]{1,0:T(8,128)S(1)}, f32[32,128]{1,0:T(8,128)S(1)}, u32[]{:S(2)}, u32[]{:S(2)}) %collective-permute-start.3) | collective-permute-done | bytes 16416 | tf_op jit(solution)/shard_map/ppermute | solution.py:501
  17.0 0.0 collective-permute-done.got_a
  17.0 0.0 collective-permute-done.1.got_b
  17.0 2.2 %rim.1 = (f32[4,4,64,512]{3,2,1,0:T(8,128)}, f32[4,4,64,512]{3,2,1,0:T(8,128)}, f32[4,4,64,512]{3,2,1,0:T(8,128)S(1)}, f32[4,4,64,512]{3,2,1,0:T(8,128)S(1)}) custom-call(f32[32,512]{1,0:T(8,128)S(1)} %collective-permute-done.got_a, f32[136,128]{1,0:T(8,128)S(1)} %collective-permute-done.1.got_b, ...), custom_call_target="tpu_custom_call", output_to_operand_aliasing={{2}: (8, {}), {3}: (9, {})} | custom-call | flops 500000 | bytes 3000000 | tf_op jit(solution)/shard_map/rim/pallas_call | solution.py:523
Async XLA Ops:
  0.6 10.8 %copy-start.4 = (s32[4,64,512]{2,1,0:T(8,128)S(1)}, s32[4,64,512]{2,1,0:T(8,128)}, u32[]{:S(2)}) copy-start(s32[4,64,512]{2,1,0:T(8,128)} %north_flags.3) | copy-start | bytes 1572868
  0.6 10.8 %copy-start.3 = (s32[4,64,512]{2,1,0:T(8,128)S(1)}, s32[4,64,512]{2,1,0:T(8,128)}, u32[]{:S(2)}) copy-start(s32[4,64,512]{2,1,0:T(8,128)} %east_flags.3) | copy-start | bytes 1572868
  0.7 10.8 %copy-start.2 = (s32[4,64,512]{2,1,0:T(8,128)S(1)}, s32[4,64,512]{2,1,0:T(8,128)}, u32[]{:S(2)}) copy-start(s32[4,64,512]{2,1,0:T(8,128)} %scalar_flags.3) | copy-start | bytes 1572868
  0.7 10.8 %copy-start.1 = (f32[4,4,64,512]{3,2,1,0:T(8,128)S(1)}, f32[4,4,64,512]{3,2,1,0:T(8,128)}, u32[]{:S(2)}) copy-start(f32[4,4,64,512]{3,2,1,0:T(8,128)} %raw_cur.1) | copy-start | bytes 6291460
  0.7 10.8 %copy-start = (f32[4,4,64,512]{3,2,1,0:T(8,128)S(1)}, f32[4,4,64,512]{3,2,1,0:T(8,128)}, u32[]{:S(2)}) copy-start(f32[4,4,64,512]{3,2,1,0:T(8,128)} %raw_bef.1) | copy-start | bytes 6291460
  4.0 13.1 %collective-permute-start.1 = (f32[136,128]{1,0:T(8,128)S(1)}, f32[136,128]{1,0:T(8,128)S(1)}, u32[]{:S(2)}, u32[]{:S(2)}) collective-permute-start(f32[136,128]{1,0:T(8,128)S(1)} %get-tuple-element.15), channel_id=1, source_target_pairs={{0,30},{1,31},{2,28},{3,29},{4,26},{5,27},{6,24},{7,25},{8,22},{9,... | collective-permute-start | bytes 208904 | tf_op jit(solution)/shard_map/ppermute | solution.py:498
  9.4 7.6 %collective-permute-start = (f32[32,512]{1,0:T(8,128)S(1)}, f32[32,512]{1,0:T(8,128)S(1)}, u32[]{:S(2)}, u32[]{:S(2)}) collective-permute-start(f32[32,512]{1,0:T(8,128)S(1)} %get-tuple-element.14), channel_id=1, source_target_pairs={{0,1},{1,0},{2,3},{3,2},{4,5},{5,4},{6,7},{7,6},{8,9},{9,8},{10,11... | collective-permute-start | bytes 196616 | tf_op jit(solution)/shard_map/ppermute | solution.py:499
  11.0 4.5 %collective-permute-start.2 = (f32[32,128]{1,0:T(8,128)S(1)}, f32[32,128]{1,0:T(8,128)S(1)}, u32[]{:S(2)}, u32[]{:S(2)}) collective-permute-start(f32[32,128]{1,0:T(8,128)S(1)} %get-tuple-element.16), channel_id=1, source_target_pairs={{0,30},{2,0},{4,2},{6,4},{8,6},{10,8},{12,10},{14,12},{16,14},{18,... | collective-permute-start | bytes 49160 | tf_op jit(solution)/shard_map/ppermute | solution.py:500
  11.2 5.9 %collective-permute-start.3 = (f32[32,128]{1,0:T(8,128)S(1)}, f32[32,128]{1,0:T(8,128)S(1)}, u32[]{:S(2)}, u32[]{:S(2)}) collective-permute-start(f32[32,128]{1,0:T(8,128)S(1)} %get-tuple-element.17), channel_id=1, source_target_pairs={{0,2},{2,4},{4,6},{6,8},{8,10},{10,12},{12,14},{14,16},{16,18},{18... | collective-permute-start | bytes 49160 | tf_op jit(solution)/shard_map/ppermute | solution.py:501

commit v4 on v3

--- a/solution.py
+++ b/solution.py
@@ -167,7 +167,11 @@
     back = LANES - 1 - lane
     even = lat % 2 == 0
     is_top = lat == n_lat - 1
-    puts = [(pay_b, pl.ds(2 * ROWS * n_tiles, SUBS), slice(None), zeros)]
+    puts = [
+        (ref, pl.ds(r, SUBS), slice(None), zeros)
+        for ref, used in ((pay_b, 2 * ROWS * n_tiles), (pay_west, height // 2), (pay_east, height // 2))
+        for r in range(used, ref.shape[0], SUBS)
+    ]
     into_b, folded = [], []
     for j in range(n_tiles):
         cols = pl.ds(j * LANES, LANES)
@@ -314,25 +318,25 @@
                         puts.append((bef_v, (f, l, j, rows), raw_bef[f, l, rows, cols] * masks[mask_of(f)]))
                 yield puts
 
-    for c in range(2):
-        for puts in masking(c):
-            store(puts)
-
-    def two_chunks(i, carry):
-        units = [unit(2 * i + k, l, range(FIELDS)) for k in range(2) for l in range(LEVELS)]
-        later = [masking(jnp.minimum(2 * i + 2 + k, n_chunks - 1)) for k in range(2)]
-        per_chunk = len(units) // 2
+    for puts in masking(0):
+        store(puts)
+
+    chunks = 4 if n_chunks % 4 == 0 else 1
+
+    def some_chunks(i, carry):
+        units = [unit(chunks * i + k, l, range(FIELDS)) for k in range(chunks) for l in range(LEVELS)]
+        later = [masking(jnp.minimum(chunks * i + k + 1, n_chunks - 1)) for k in range(chunks)]
         for t in range(len(units) + 2):
             puts = []
             for u in (t, t - 1, t - 2):
                 if 0 <= u < len(units):
                     puts += next(units[u])
             if t < len(units):
-                puts += next(later[t // per_chunk]) + next(later[t // per_chunk])
+                puts += next(later[t // LEVELS]) + next(later[t // LEVELS])
             store(puts)
         return carry
 
-    lax.fori_loop(0, n_chunks // 2, two_chunks, 0)
+    lax.fori_loop(0, n_chunks // chunks, some_chunks, 0)
 
 
 def rim_kernel(
@@ -384,7 +388,7 @@
                 + coef(coef_south, 4 + h) * south[3]
             )
 
-    for side, (got, coef) in enumerate(((got_west[...], coef_west), (got_east[...], coef_east))):
+    for side, (got, coef) in enumerate(((got_west[pl.ds(0, height // 2), :], coef_west), (got_east[pl.ds(0, height // 2), :], coef_east))):
         for part in range(2):
             rows = pl.ds(part * (height // 2), height // 2)
             x = got if part == 0 else pltpu.roll(got, LANES // 2, 1)
@@ -457,14 +461,16 @@
     state = (FIELDS, LEVELS, height, width)
     apart = (LEVELS, width // LANES, height + SUBS, LANES)
 
+    wide = 2 * ROWS * (width // LANES)
+
     def vmem(*shape):
         return pltpu.VMEM(shape, f32)
 
     edges = pl.pallas_call(
         functools.partial(edges_kernel, n_lat),
         out_shape=[
-            vmem(2 * ROWS, width), vmem(2 * ROWS * (width // LANES) + SUBS, LANES),
-            vmem(height // 2, LANES), vmem(height // 2, LANES),
+            vmem(2 * ROWS, width), vmem(wide + 2 * SUBS, LANES),
+            vmem(max(wide + SUBS, height // 2), LANES), vmem(max(wide + SUBS, height // 2), LANES),
             vmem(2 * ROWS + SUBS, width), vmem(3 * ROWS, width), vmem(height, LANES), vmem(height, LANES),
         ],
         in_specs=[ANY] * 5,

time: 19.4 us -> 18.7 us (0.964)
  the two profiles are of different devices: /device:TPU:0 before, /device:TPU:1 now
where the time goes in v4:
time: 18.7 us; the launch traced here: 18.6 us
  Pallas kernels  9.11 us (49%)
  starting transfers between devices  8.69 us (46%)
  between operations  0.73 us (4%)
    ppermute x1, starting transfers between devices, shards(): got_b = lax.ppermute(pay_b, ('lon', 'lat'), pairs_b)  5.7 us
    pallas_call x1, Pallas kernels, shards(): pl.pallas_call(functools.partial(inner_kernel, height * n_lat), out_shape...  3.64 us
    pallas_call x1, Pallas kernels, shards(): pl.pallas_call(functools.partial(edges_kernel, n_lat), out_shape=[vmem(2...  3.28 us
    pallas_call x1, Pallas kernels, shards(): pl.pallas_call(rim_kernel, out_shape=[pltpu.HBM(state, f32), pltpu.HBM(st...  2.19 us
    ppermute x1, starting transfers between devices, shards(): lax.ppermute(pay_east, 'lon', [(i, (i + 1) % n_lon) for i in lons])  1.74 us
    ppermute x1, starting transfers between devices, shards(): got_a = lax.ppermute(pay_a, ('lon', 'lat'), pairs_a)  1.24 us
  transfers between devices with their start and end apart: 4, of which 0 were waited for; matrix products, arithmetic and copies ran while one was open for 0% of the time, Pallas kernels for 20%

profile of v4, /device:TPU:1, one launch (start us, length us, event | category | flops | bytes accessed | tf_op | source)
XLA Modules:
  0.0 18.6 jit_solution(2719871198291112271)
XLA Ops:
  0.6 0.0 copy-start.4
  0.6 0.0 copy-start.3
  0.7 0.0 copy-start.2
  0.7 0.0 copy-start.1
  0.7 0.0 copy-start
  0.7 3.3 %edges.1 = (f32[32,512]{1,0:T(8,128)S(1)}, f32[144,128]{1,0:T(8,128)S(1)}, f32[136,128]{1,0:T(8,128)S(1)}, f32[136,128]{1,0:T(8,128)S(1)}, f32[40,512]{1,0:T(8,1...) custom-call(f32[4,4,64,512]{3,2,1,0:T(8,128)} %raw_bef.1, ...), custom_call_target="tpu_custom_call" | custom-call | flops 500000 | bytes 3600000 | tf_op jit(solution)/shard_map/edges/pallas_call | solution.py:469
  4.0 5.7 %collective-permute-start.1 = (f32[144,128]{1,0:T(8,128)S(1)}, f32[144,128]{1,0:T(8,128)S(1)}, u32[]{:S(2)}, u32[]{:S(2)}) collective-permute-start(f32[144,128]{1,0:T(8,128)S(1)} %get-tuple-element.15), channel_id=1, source_target_pairs={{0,30},{1,31},{2,28},{3,29},{4,26},{5,27},{6,24},{7,25},{8,22},{9,... | collective-permute-start | bytes 221192 | tf_op jit(solution)/shard_map/ppermute | solution.py:504
  9.7 0.0 collective-permute-start.2
  9.7 1.7 %collective-permute-start.3 = (f32[136,128]{1,0:T(8,128)S(1)}, f32[136,128]{1,0:T(8,128)S(1)}, u32[]{:S(2)}, u32[]{:S(2)}) collective-permute-start(f32[136,128]{1,0:T(8,128)S(1)} %get-tuple-element.17), channel_id=1, source_target_pairs={{0,2},{2,4},{4,6},{6,8},{8,10},{10,12},{12,14},{14,16},{16,18},{18... | collective-permute-start | bytes 208904 | tf_op jit(solution)/shard_map/ppermute | solution.py:507
  11.4 1.2 %collective-permute-start = (f32[32,512]{1,0:T(8,128)S(1)}, f32[32,512]{1,0:T(8,128)S(1)}, u32[]{:S(2)}, u32[]{:S(2)}) collective-permute-start(f32[32,512]{1,0:T(8,128)S(1)} %get-tuple-element.14), channel_id=1, source_target_pairs={{0,1},{1,0},{2,3},{3,2},{4,5},{5,4},{6,7},{7,6},{8,9},{9,8},{10,11... | collective-permute-start | bytes 196616 | tf_op jit(solution)/shard_map/ppermute | solution.py:505
  12.7 0.0 copy-done.4
  12.7 0.0 copy-done.3
  12.7 0.0 copy-done.2
  12.7 0.0 copy-done.1
  12.7 0.0 copy-done
  12.7 3.6 %inner.1 = (f32[4,4,64,512]{3,2,1,0:T(8,128)S(1)}, f32[4,4,64,512]{3,2,1,0:T(8,128)S(1)}) custom-call(f32[4,4,64,512]{3,2,1,0:T(8,128)S(1)} %copy-done, f32[4,4,64,512]{3,2,1,0:T(8,128)S(1)} %copy-done.1, s32[4,64,512]{2,1,0:T(8,128)S(1)} %copy-done.2, s32[4,64,512]{2,1,0:T(8,128)S(1)} %copy-done.3, s32[4,64,512]{2,1,0:T(8,128)S(1)} %copy-done.4), custom_call_target="tpu_custom_call" | custom-call | flops 20000000 | bytes 9000000 | tf_op jit(solution)/shard_map/inner/pallas_call | solution.py:509
  16.3 0.0 collective-permute-done.got_a
  16.3 0.0 collective-permute-done.2.got_east
  16.4 0.0 collective-permute-done.3.got_west
  16.4 0.0 collective-permute-done.1.got_b
  16.4 2.2 %rim.1 = (f32[4,4,64,512]{3,2,1,0:T(8,128)}, f32[4,4,64,512]{3,2,1,0:T(8,128)}, f32[4,4,64,512]{3,2,1,0:T(8,128)S(1)}, f32[4,4,64,512]{3,2,1,0:T(8,128)S(1)}) custom-call(f32[32,512]{1,0:T(8,128)S(1)} %collective-permute-done.got_a, f32[144,128]{1,0:T(8,128)S(1)} %collective-permute-done.1.got_b, ...), custom_call_target="tpu_custom_call", output_to_operand_aliasing={{2}: (8, {}), {3}: (9, {})} | custom-call | flops 500000 | bytes 3000000 | tf_op jit(solution)/shard_map/rim/pallas_call | solution.py:529
Async XLA Ops:
  0.6 12.0 %copy-start.4 = (s32[4,64,512]{2,1,0:T(8,128)S(1)}, s32[4,64,512]{2,1,0:T(8,128)}, u32[]{:S(2)}) copy-start(s32[4,64,512]{2,1,0:T(8,128)} %north_flags.3) | copy-start | bytes 1572868
  0.6 12.0 %copy-start.3 = (s32[4,64,512]{2,1,0:T(8,128)S(1)}, s32[4,64,512]{2,1,0:T(8,128)}, u32[]{:S(2)}) copy-start(s32[4,64,512]{2,1,0:T(8,128)} %east_flags.3) | copy-start | bytes 1572868
  0.7 12.0 %copy-start.2 = (s32[4,64,512]{2,1,0:T(8,128)S(1)}, s32[4,64,512]{2,1,0:T(8,128)}, u32[]{:S(2)}) copy-start(s32[4,64,512]{2,1,0:T(8,128)} %scalar_flags.3) | copy-start | bytes 1572868
  0.7 12.0 %copy-start.1 = (f32[4,4,64,512]{3,2,1,0:T(8,128)S(1)}, f32[4,4,64,512]{3,2,1,0:T(8,128)}, u32[]{:S(2)}) copy-start(f32[4,4,64,512]{3,2,1,0:T(8,128)} %raw_cur.1) | copy-start | bytes 6291460
  0.7 12.0 %copy-start = (f32[4,4,64,512]{3,2,1,0:T(8,128)S(1)}, f32[4,4,64,512]{3,2,1,0:T(8,128)}, u32[]{:S(2)}) copy-start(f32[4,4,64,512]{3,2,1,0:T(8,128)} %raw_bef.1) | copy-start | bytes 6291460
  4.0 12.4 %collective-permute-start.1 = (f32[144,128]{1,0:T(8,128)S(1)}, f32[144,128]{1,0:T(8,128)S(1)}, u32[]{:S(2)}, u32[]{:S(2)}) collective-permute-start(f32[144,128]{1,0:T(8,128)S(1)} %get-tuple-element.15), channel_id=1, source_target_pairs={{0,30},{1,31},{2,28},{3,29},{4,26},{5,27},{6,24},{7,25},{8,22},{9,... | collective-permute-start | bytes 221192 | tf_op jit(solution)/shard_map/ppermute | solution.py:504
  9.7 6.7 %collective-permute-start.2 = (f32[136,128]{1,0:T(8,128)S(1)}, f32[136,128]{1,0:T(8,128)S(1)}, u32[]{:S(2)}, u32[]{:S(2)}) collective-permute-start(f32[136,128]{1,0:T(8,128)S(1)} %get-tuple-element.16), channel_id=1, source_target_pairs={{0,30},{2,0},{4,2},{6,4},{8,6},{10,8},{12,10},{14,12},{16,14},{18,... | collective-permute-start | bytes 208904 | tf_op jit(solution)/shard_map/ppermute | solution.py:506
  9.7 6.7 %collective-permute-start.3 = (f32[136,128]{1,0:T(8,128)S(1)}, f32[136,128]{1,0:T(8,128)S(1)}, u32[]{:S(2)}, u32[]{:S(2)}) collective-permute-start(f32[136,128]{1,0:T(8,128)S(1)} %get-tuple-element.17), channel_id=1, source_target_pairs={{0,2},{2,4},{4,6},{6,8},{8,10},{10,12},{12,14},{14,16},{16,18},{18... | collective-permute-start | bytes 208904 | tf_op jit(solution)/shard_map/ppermute | solution.py:507
  11.4 4.9 %collective-permute-start = (f32[32,512]{1,0:T(8,128)S(1)}, f32[32,512]{1,0:T(8,128)S(1)}, u32[]{:S(2)}, u32[]{:S(2)}) collective-permute-start(f32[32,512]{1,0:T(8,128)S(1)} %get-tuple-element.14), channel_id=1, source_target_pairs={{0,1},{1,0},{2,3},{3,2},{4,5},{5,4},{6,7},{7,6},{8,9},{9,8},{10,11... | collective-permute-start | bytes 196616 | tf_op jit(solution)/shard_map/ppermute | solution.py:505

commit v5 on v4

--- a/solution.py
+++ b/solution.py
@@ -71,7 +71,7 @@
     lane = lane_ids((SUBS, LANES))
     sub = row_ids((SUBS, LANES))
 
-    for copy in copies[:10]:
+    for copy in copies[:5]:
         copy.wait()
 
     base, level = lane & (ROWS - 1), lane & (LEVELS - 1)
@@ -107,11 +107,23 @@
 
     in_pres = (lane >= 2 * ROWS + 2 * LEVELS) & (lane < 2 * ROWS + 3 * LEVELS)
     going_west, going_east, coefs_west, coefs_east = [], [], [], []
+
+    def put_column(pay, coef, going, coefs):
+        half = len(tiles) // 2
+        folded = [jnp.where(lane < LANES // 2, going[r], pltpu.roll(going[r + half], LANES // 2, 1)) for r in range(half)]
+        for r in tiles:
+            coef[pl.ds(r * SUBS, SUBS), :] = coefs[r]
+            if r < half:
+                pay[pl.ds(r * SUBS, SUBS), :] = folded[r]
+
     for fm, both, pres, _ in col_pack(0, 0):
         both = both * fm
         moved = pltpu.roll(both, ROWS, 1)
         going_west.append(both + pres)
         coefs_west.append(twice_step * jnp.where(lane < ROWS, fm, jnp.where(lane < 2 * ROWS, moved, -moved)))
+    put_column(pay_west, coef_west, going_west, coefs_west)
+    for copy in copies[5:10]:
+        copy.wait()
     for fm, both, mu, u in col_pack(1, LANES - 1):
         s, dm = speed_coef * u * mu, diffuse_coef * mu
         own = both * fm * jnp.where(lane < ROWS, s, dm)
@@ -121,19 +133,7 @@
         coefs_east.append(
             jnp.where(lane < 2 * ROWS, face, jnp.where(in_pres, -twice_step * gravity * mu, 0.0))
         )
-    half = len(tiles) // 2
-    folded = [
-        [jnp.where(lane < LANES // 2, x[r], pltpu.roll(x[r + half], LANES // 2, 1)) for r in range(half)]
-        for x in (going_west, going_east)
-    ]
-    for r in tiles:
-        rows = pl.ds(r * SUBS, SUBS)
-        coef_west[rows, :] = coefs_west[r]
-        coef_east[rows, :] = coefs_east[r]
-        if r < half:
-            pay_west[rows, :] = folded[0][r]
-            pay_east[rows, :] = folded[1][r]
-
+    put_column(pay_east, coef_east, going_east, coefs_east)
     for copy in copies[10:]:
         copy.wait()
 

time: 18.7 us -> 18.3 us (0.979)
  Pallas kernels: 9.11 us -> 8.74 us
    pallas_call x1, Pallas kernels: 3.28 us -> 2.9 us  [shards(): pl.pallas_call(functools.partial(edges_kernel, n_lat), out_shape=[vmem(2...]
where the time goes in v5:
time: 18.3 us; the launch traced here: 18.2 us
  Pallas kernels  8.74 us (48%)
  starting transfers between devices  8.69 us (47%)
  between operations  0.73 us (4%)
    ppermute x1, starting transfers between devices, shards(): got_b = lax.ppermute(pay_b, ('lon', 'lat'), pairs_b)  5.7 us
    pallas_call x1, Pallas kernels, shards(): pl.pallas_call(functools.partial(inner_kernel, height * n_lat), out_shape...  3.64 us
    pallas_call x1, Pallas kernels, shards(): pl.pallas_call(functools.partial(edges_kernel, n_lat), out_shape=[vmem(2...  2.9 us
    pallas_call x1, Pallas kernels, shards(): pl.pallas_call(rim_kernel, out_shape=[pltpu.HBM(state, f32), pltpu.HBM(st...  2.19 us
    ppermute x1, starting transfers between devices, shards(): lax.ppermute(pay_east, 'lon', [(i, (i + 1) % n_lon) for i in lons])  1.74 us
    ppermute x1, starting transfers between devices, shards(): got_a = lax.ppermute(pay_a, ('lon', 'lat'), pairs_a)  1.24 us
  transfers between devices with their start and end apart: 4, of which 0 were waited for; matrix products, arithmetic and copies ran while one was open for 0% of the time, Pallas kernels for 20%

profile of v5, /device:TPU:1, one launch (start us, length us, event | category | flops | bytes accessed | tf_op | source)
XLA Modules:
  0.0 18.2 jit_solution(4605424125556134995)
XLA Ops:
  0.6 0.0 copy-start.4
  0.6 0.0 copy-start.3
  0.7 0.0 copy-start.2
  0.7 0.0 copy-start.1
  0.7 0.0 copy-start
  0.7 2.9 %edges.1 = (f32[32,512]{1,0:T(8,128)S(1)}, f32[144,128]{1,0:T(8,128)S(1)}, f32[136,128]{1,0:T(8,128)S(1)}, f32[136,128]{1,0:T(8,128)S(1)}, f32[40,512]{1,0:T(8,1...) custom-call(f32[4,4,64,512]{3,2,1,0:T(8,128)} %raw_bef.1, ...), custom_call_target="tpu_custom_call" | custom-call | flops 500000 | bytes 3600000 | tf_op jit(solution)/shard_map/edges/pallas_call | solution.py:469
  3.6 5.7 %collective-permute-start.1 = (f32[144,128]{1,0:T(8,128)S(1)}, f32[144,128]{1,0:T(8,128)S(1)}, u32[]{:S(2)}, u32[]{:S(2)}) collective-permute-start(f32[144,128]{1,0:T(8,128)S(1)} %get-tuple-element.15), channel_id=1, source_target_pairs={{0,30},{1,31},{2,28},{3,29},{4,26},{5,27},{6,24},{7,25},{8,22},{9,... | collective-permute-start | bytes 221192 | tf_op jit(solution)/shard_map/ppermute | solution.py:504
  9.3 0.0 collective-permute-start.2
  9.3 1.7 %collective-permute-start.3 = (f32[136,128]{1,0:T(8,128)S(1)}, f32[136,128]{1,0:T(8,128)S(1)}, u32[]{:S(2)}, u32[]{:S(2)}) collective-permute-start(f32[136,128]{1,0:T(8,128)S(1)} %get-tuple-element.17), channel_id=1, source_target_pairs={{0,2},{2,4},{4,6},{6,8},{8,10},{10,12},{12,14},{14,16},{16,18},{18... | collective-permute-start | bytes 208904 | tf_op jit(solution)/shard_map/ppermute | solution.py:507
  11.0 1.2 %collective-permute-start = (f32[32,512]{1,0:T(8,128)S(1)}, f32[32,512]{1,0:T(8,128)S(1)}, u32[]{:S(2)}, u32[]{:S(2)}) collective-permute-start(f32[32,512]{1,0:T(8,128)S(1)} %get-tuple-element.14), channel_id=1, source_target_pairs={{0,1},{1,0},{2,3},{3,2},{4,5},{5,4},{6,7},{7,6},{8,9},{9,8},{10,11... | collective-permute-start | bytes 196616 | tf_op jit(solution)/shard_map/ppermute | solution.py:505
  12.3 0.0 copy-done.4
  12.3 0.0 copy-done.3
  12.3 0.0 copy-done.2
  12.3 0.0 copy-done.1
  12.3 0.0 copy-done
  12.3 3.6 %inner.1 = (f32[4,4,64,512]{3,2,1,0:T(8,128)S(1)}, f32[4,4,64,512]{3,2,1,0:T(8,128)S(1)}) custom-call(f32[4,4,64,512]{3,2,1,0:T(8,128)S(1)} %copy-done, f32[4,4,64,512]{3,2,1,0:T(8,128)S(1)} %copy-done.1, s32[4,64,512]{2,1,0:T(8,128)S(1)} %copy-done.2, s32[4,64,512]{2,1,0:T(8,128)S(1)} %copy-done.3, s32[4,64,512]{2,1,0:T(8,128)S(1)} %copy-done.4), custom_call_target="tpu_custom_call" | custom-call | flops 20000000 | bytes 9000000 | tf_op jit(solution)/shard_map/inner/pallas_call | solution.py:509
  16.0 0.0 collective-permute-done.got_a
  16.0 0.0 collective-permute-done.2.got_east
  16.0 0.0 collective-permute-done.3.got_west
  16.0 0.0 collective-permute-done.1.got_b
  16.0 2.2 %rim.1 = (f32[4,4,64,512]{3,2,1,0:T(8,128)}, f32[4,4,64,512]{3,2,1,0:T(8,128)}, f32[4,4,64,512]{3,2,1,0:T(8,128)S(1)}, f32[4,4,64,512]{3,2,1,0:T(8,128)S(1)}) custom-call(f32[32,512]{1,0:T(8,128)S(1)} %collective-permute-done.got_a, f32[144,128]{1,0:T(8,128)S(1)} %collective-permute-done.1.got_b, ...), custom_call_target="tpu_custom_call", output_to_operand_aliasing={{2}: (8, {}), {3}: (9, {})} | custom-call | flops 500000 | bytes 3000000 | tf_op jit(solution)/shard_map/rim/pallas_call | solution.py:529
Async XLA Ops:
  0.6 11.7 %copy-start.4 = (s32[4,64,512]{2,1,0:T(8,128)S(1)}, s32[4,64,512]{2,1,0:T(8,128)}, u32[]{:S(2)}) copy-start(s32[4,64,512]{2,1,0:T(8,128)} %north_flags.3) | copy-start | bytes 1572868
  0.6 11.6 %copy-start.3 = (s32[4,64,512]{2,1,0:T(8,128)S(1)}, s32[4,64,512]{2,1,0:T(8,128)}, u32[]{:S(2)}) copy-start(s32[4,64,512]{2,1,0:T(8,128)} %east_flags.3) | copy-start | bytes 1572868
  0.7 11.6 %copy-start.2 = (s32[4,64,512]{2,1,0:T(8,128)S(1)}, s32[4,64,512]{2,1,0:T(8,128)}, u32[]{:S(2)}) copy-start(s32[4,64,512]{2,1,0:T(8,128)} %scalar_flags.3) | copy-start | bytes 1572868
  0.7 11.6 %copy-start.1 = (f32[4,4,64,512]{3,2,1,0:T(8,128)S(1)}, f32[4,4,64,512]{3,2,1,0:T(8,128)}, u32[]{:S(2)}) copy-start(f32[4,4,64,512]{3,2,1,0:T(8,128)} %raw_cur.1) | copy-start | bytes 6291460
  0.7 11.6 %copy-start = (f32[4,4,64,512]{3,2,1,0:T(8,128)S(1)}, f32[4,4,64,512]{3,2,1,0:T(8,128)}, u32[]{:S(2)}) copy-start(f32[4,4,64,512]{3,2,1,0:T(8,128)} %raw_bef.1) | copy-start | bytes 6291460
  3.6 12.4 %collective-permute-start.1 = (f32[144,128]{1,0:T(8,128)S(1)}, f32[144,128]{1,0:T(8,128)S(1)}, u32[]{:S(2)}, u32[]{:S(2)}) collective-permute-start(f32[144,128]{1,0:T(8,128)S(1)} %get-tuple-element.15), channel_id=1, source_target_pairs={{0,30},{1,31},{2,28},{3,29},{4,26},{5,27},{6,24},{7,25},{8,22},{9,... | collective-permute-start | bytes 221192 | tf_op jit(solution)/shard_map/ppermute | solution.py:504
  9.3 6.7 %collective-permute-start.2 = (f32[136,128]{1,0:T(8,128)S(1)}, f32[136,128]{1,0:T(8,128)S(1)}, u32[]{:S(2)}, u32[]{:S(2)}) collective-permute-start(f32[136,128]{1,0:T(8,128)S(1)} %get-tuple-element.16), channel_id=1, source_target_pairs={{0,30},{2,0},{4,2},{6,4},{8,6},{10,8},{12,10},{14,12},{16,14},{18,... | collective-permute-start | bytes 208904 | tf_op jit(solution)/shard_map/ppermute | solution.py:506
  9.3 6.7 %collective-permute-start.3 = (f32[136,128]{1,0:T(8,128)S(1)}, f32[136,128]{1,0:T(8,128)S(1)}, u32[]{:S(2)}, u32[]{:S(2)}) collective-permute-start(f32[136,128]{1,0:T(8,128)S(1)} %get-tuple-element.17), channel_id=1, source_target_pairs={{0,2},{2,4},{4,6},{6,8},{8,10},{10,12},{12,14},{14,16},{16,18},{18... | collective-permute-start | bytes 208904 | tf_op jit(solution)/shard_map/ppermute | solution.py:507
  11.0 4.9 %collective-permute-start = (f32[32,512]{1,0:T(8,128)S(1)}, f32[32,512]{1,0:T(8,128)S(1)}, u32[]{:S(2)}, u32[]{:S(2)}) collective-permute-start(f32[32,512]{1,0:T(8,128)S(1)} %get-tuple-element.14), channel_id=1, source_target_pairs={{0,1},{1,0},{2,3},{3,2},{4,5},{5,4},{6,7},{7,6},{8,9},{9,8},{10,11... | collective-permute-start | bytes 196616 | tf_op jit(solution)/shard_map/ppermute | solution.py:505

commit v6 on v5

--- a/solution.py
+++ b/solution.py
@@ -321,7 +321,7 @@
     for puts in masking(0):
         store(puts)
 
-    chunks = 4 if n_chunks % 4 == 0 else 1
+    chunks = next(k for k in (8, 4, 2, 1) if n_chunks % k == 0)
 
     def some_chunks(i, carry):
         units = [unit(chunks * i + k, l, range(FIELDS)) for k in range(chunks) for l in range(LEVELS)]

time: 18.3 us -> 17.9 us (0.978)
  the two profiles are of different devices: /device:TPU:1 before, /device:TPU:0 now
where the time goes in v6:
time: 17.9 us; the launch traced here: 17.8 us
  Pallas kernels  8.08 us (45%)
  starting transfers between devices  7.68 us (43%)
  waiting for transfers between devices  1.26 us (7%)
  between operations  0.72 us (4%)
    ppermute x1, starting transfers between devices, shards(): got_b = lax.ppermute(pay_b, ('lon', 'lat'), pairs_b)  5.48 us
    pallas_call x1, Pallas kernels, shards(): pl.pallas_call(functools.partial(inner_kernel, height * n_lat), out_shape...  3 us
    pallas_call x1, Pallas kernels, shards(): pl.pallas_call(functools.partial(edges_kernel, n_lat), out_shape=[vmem(2...  2.9 us
    pallas_call x1, Pallas kernels, shards(): pl.pallas_call(rim_kernel, out_shape=[pltpu.HBM(state, f32), pltpu.HBM(st...  2.18 us
    ppermute x1, starting transfers between devices, shards(): got_a = lax.ppermute(pay_a, ('lon', 'lat'), pairs_a)  1.52 us
    ppermute x1, waiting for transfers between devices, shards(): lax.ppermute(pay_east, 'lon', [(i, (i + 1) % n_lon) for i in lons])  1.25 us
    ppermute x1, starting transfers between devices, shards(): lax.ppermute(pay_east, 'lon', [(i, (i + 1) % n_lon) for i in lons])  0.61 us
  transfers between devices with their start and end apart: 4, of which 1 were waited for; matrix products, arithmetic and copies ran while one was open for 0% of the time, Pallas kernels for 17%

profile of v6, /device:TPU:0, one launch (start us, length us, event | category | flops | bytes accessed | tf_op | source)
XLA Modules:
  0.0 17.8 jit_solution(2129370130829249820)
XLA Ops:
  0.6 0.0 copy-start.4
  0.6 0.0 copy-start.3
  0.7 0.0 copy-start.2
  0.7 0.0 copy-start.1
  0.7 0.0 copy-start
  0.7 2.9 %edges.1 = (f32[32,512]{1,0:T(8,128)S(1)}, f32[144,128]{1,0:T(8,128)S(1)}, f32[136,128]{1,0:T(8,128)S(1)}, f32[136,128]{1,0:T(8,128)S(1)}, f32[40,512]{1,0:T(8,1...) custom-call(f32[4,4,64,512]{3,2,1,0:T(8,128)} %raw_bef.1, ...), custom_call_target="tpu_custom_call" | custom-call | flops 500000 | bytes 3600000 | tf_op jit(solution)/shard_map/edges/pallas_call | solution.py:469
  3.6 5.5 %collective-permute-start.1 = (f32[144,128]{1,0:T(8,128)S(1)}, f32[144,128]{1,0:T(8,128)S(1)}, u32[]{:S(2)}, u32[]{:S(2)}) collective-permute-start(f32[144,128]{1,0:T(8,128)S(1)} %get-tuple-element.15), channel_id=1, source_target_pairs={{0,30},{1,31},{2,28},{3,29},{4,26},{5,27},{6,24},{7,25},{8,22},{9,... | collective-permute-start | bytes 221192 | tf_op jit(solution)/shard_map/ppermute | solution.py:504
  9.1 0.1 collective-permute-start.2
  9.1 0.6 %collective-permute-start.3 = (f32[136,128]{1,0:T(8,128)S(1)}, f32[136,128]{1,0:T(8,128)S(1)}, u32[]{:S(2)}, u32[]{:S(2)}) collective-permute-start(f32[136,128]{1,0:T(8,128)S(1)} %get-tuple-element.17), channel_id=1, source_target_pairs={{0,2},{2,4},{4,6},{6,8},{8,10},{10,12},{12,14},{14,16},{16,18},{18... | collective-permute-start | bytes 208904 | tf_op jit(solution)/shard_map/ppermute | solution.py:507
  9.8 1.5 %collective-permute-start = (f32[32,512]{1,0:T(8,128)S(1)}, f32[32,512]{1,0:T(8,128)S(1)}, u32[]{:S(2)}, u32[]{:S(2)}) collective-permute-start(f32[32,512]{1,0:T(8,128)S(1)} %get-tuple-element.14), channel_id=1, source_target_pairs={{0,1},{1,0},{2,3},{3,2},{4,5},{5,4},{6,7},{7,6},{8,9},{9,8},{10,11... | collective-permute-start | bytes 196616 | tf_op jit(solution)/shard_map/ppermute | solution.py:505
  11.3 0.0 copy-done.4
  11.3 0.0 copy-done.3
  11.3 0.0 copy-done.2
  11.3 0.0 copy-done.1
  11.3 0.0 copy-done
  11.3 3.0 %inner.1 = (f32[4,4,64,512]{3,2,1,0:T(8,128)S(1)}, f32[4,4,64,512]{3,2,1,0:T(8,128)S(1)}) custom-call(f32[4,4,64,512]{3,2,1,0:T(8,128)S(1)} %copy-done, f32[4,4,64,512]{3,2,1,0:T(8,128)S(1)} %copy-done.1, s32[4,64,512]{2,1,0:T(8,128)S(1)} %copy-done.2, s32[4,64,512]{2,1,0:T(8,128)S(1)} %copy-done.3, s32[4,64,512]{2,1,0:T(8,128)S(1)} %copy-done.4), custom_call_target="tpu_custom_call" | custom-call | flops 20000000 | bytes 9000000 | tf_op jit(solution)/shard_map/inner/pallas_call | solution.py:509
  14.3 0.0 collective-permute-done.got_a
  14.3 0.0 collective-permute-done.2.got_east
  14.3 1.2 %collective-permute-done.3.got_west = f32[136,128]{1,0:T(8,128)S(1)} collective-permute-done((f32[136,128]{1,0:T(8,128)S(1)}, f32[136,128]{1,0:T(8,128)S(1)}, u32[]{:S(2)}, u32[]{:S(2)}) %collective-permute-start.3) | collective-permute-done | bytes 69664 | tf_op jit(solution)/shard_map/ppermute | solution.py:507
  15.6 0.0 collective-permute-done.1.got_b
  15.6 2.2 %rim.1 = (f32[4,4,64,512]{3,2,1,0:T(8,128)}, f32[4,4,64,512]{3,2,1,0:T(8,128)}, f32[4,4,64,512]{3,2,1,0:T(8,128)S(1)}, f32[4,4,64,512]{3,2,1,0:T(8,128)S(1)}) custom-call(f32[32,512]{1,0:T(8,128)S(1)} %collective-permute-done.got_a, f32[144,128]{1,0:T(8,128)S(1)} %collective-permute-done.1.got_b, ...), custom_call_target="tpu_custom_call", output_to_operand_aliasing={{2}: (8, {}), {3}: (9, {})} | custom-call | flops 500000 | bytes 3000000 | tf_op jit(solution)/shard_map/rim/pallas_call | solution.py:529
Async XLA Ops:
  0.6 10.6 %copy-start.4 = (s32[4,64,512]{2,1,0:T(8,128)S(1)}, s32[4,64,512]{2,1,0:T(8,128)}, u32[]{:S(2)}) copy-start(s32[4,64,512]{2,1,0:T(8,128)} %north_flags.3) | copy-start | bytes 1572868
  0.6 10.6 %copy-start.3 = (s32[4,64,512]{2,1,0:T(8,128)S(1)}, s32[4,64,512]{2,1,0:T(8,128)}, u32[]{:S(2)}) copy-start(s32[4,64,512]{2,1,0:T(8,128)} %east_flags.3) | copy-start | bytes 1572868
  0.7 10.6 %copy-start.2 = (s32[4,64,512]{2,1,0:T(8,128)S(1)}, s32[4,64,512]{2,1,0:T(8,128)}, u32[]{:S(2)}) copy-start(s32[4,64,512]{2,1,0:T(8,128)} %scalar_flags.3) | copy-start | bytes 1572868
  0.7 10.6 %copy-start.1 = (f32[4,4,64,512]{3,2,1,0:T(8,128)S(1)}, f32[4,4,64,512]{3,2,1,0:T(8,128)}, u32[]{:S(2)}) copy-start(f32[4,4,64,512]{3,2,1,0:T(8,128)} %raw_cur.1) | copy-start | bytes 6291460
  0.7 10.6 %copy-start = (f32[4,4,64,512]{3,2,1,0:T(8,128)S(1)}, f32[4,4,64,512]{3,2,1,0:T(8,128)}, u32[]{:S(2)}) copy-start(f32[4,4,64,512]{3,2,1,0:T(8,128)} %raw_bef.1) | copy-start | bytes 6291460
  3.6 12.0 %collective-permute-start.1 = (f32[144,128]{1,0:T(8,128)S(1)}, f32[144,128]{1,0:T(8,128)S(1)}, u32[]{:S(2)}, u32[]{:S(2)}) collective-permute-start(f32[144,128]{1,0:T(8,128)S(1)} %get-tuple-element.15), channel_id=1, source_target_pairs={{0,30},{1,31},{2,28},{3,29},{4,26},{5,27},{6,24},{7,25},{8,22},{9,... | collective-permute-start | bytes 221192 | tf_op jit(solution)/shard_map/ppermute | solution.py:504
  9.1 5.2 %collective-permute-start.2 = (f32[136,128]{1,0:T(8,128)S(1)}, f32[136,128]{1,0:T(8,128)S(1)}, u32[]{:S(2)}, u32[]{:S(2)}) collective-permute-start(f32[136,128]{1,0:T(8,128)S(1)} %get-tuple-element.16), channel_id=1, source_target_pairs={{0,30},{2,0},{4,2},{6,4},{8,6},{10,8},{12,10},{14,12},{16,14},{18,... | collective-permute-start | bytes 208904 | tf_op jit(solution)/shard_map/ppermute | solution.py:506
  9.1 6.4 %collective-permute-start.3 = (f32[136,128]{1,0:T(8,128)S(1)}, f32[136,128]{1,0:T(8,128)S(1)}, u32[]{:S(2)}, u32[]{:S(2)}) collective-permute-start(f32[136,128]{1,0:T(8,128)S(1)} %get-tuple-element.17), channel_id=1, source_target_pairs={{0,2},{2,4},{4,6},{6,8},{8,10},{10,12},{12,14},{14,16},{16,18},{18... | collective-permute-start | bytes 208904 | tf_op jit(solution)/shard_map/ppermute | solution.py:507
  9.8 4.5 %collective-permute-start = (f32[32,512]{1,0:T(8,128)S(1)}, f32[32,512]{1,0:T(8,128)S(1)}, u32[]{:S(2)}, u32[]{:S(2)}) collective-permute-start(f32[32,512]{1,0:T(8,128)S(1)} %get-tuple-element.14), channel_id=1, source_target_pairs={{0,1},{1,0},{2,3},{3,2},{4,5},{5,4},{6,7},{7,6},{8,9},{9,8},{10,11... | collective-permute-start | bytes 196616 | tf_op jit(solution)/shard_map/ppermute | solution.py:505
